TPU v7x, 32 devices: a whole 2x2x4 slice. The times are simulated.
32 devices in a mesh: segment: 4 (over y, core), seq: 8 (over z, x).
Axes of the slice: x: 2, y: 2, z: 4, core: 2. Of those that a mesh axis runs over, the one named last changes fastest.
Arguments:
- residual: bfloat16 [4, 1024, 8192], P('segment', 'seq'), may hold values from -6 to 6
- query_rows: bfloat16 [4, 2, 1024, 8192], P('segment', None, 'seq'), may hold values from -8 to 8
- key_rows: bfloat16 [4, 2, 1024, 1024], P('segment', None, 'seq'), may hold values from -6 to 6
- value_rows: bfloat16 [4, 2, 1024, 1024], P('segment', None, 'seq'), may hold values from -8 to 8
- pattern: int32 [4, 2, 8, 8, 8], P('segment'), may hold values from -1 to 7, as said below
Outputs:
- section_out: float32 [4, 1024, 8192], P('segment', 'seq')
Inputs may be any that keep to these rules, and one draw needn't show every extreme that they name: `pattern`: in each row (section, layer, key-value head, query block i) slot 0 holds i; the entries that are not -1 are distinct and at most i; for every section, layer and key-value head some row has all 8 slots filled.
All inputs are finite; a program needn't handle non-finite values.
Results may differ from a plain program's by a relative error of at most 0.0035.
Values may be sent and summed in bfloat16 or wider, within the bound.
No kernel may reach another device: no remote copies, remote signals or barrier semaphores. Data moves between devices by JAX's collectives and lax.ppermute only.
A program may use at most 128 MiB of HBM per device.

v0:
```python
import math

import jax
import jax.numpy as jnp
from jax import lax
from jax.sharding import PartitionSpec as P

HQ = 64
HK = 8
HD = 128
LAYERS = 2
BLOCK = 128
NSEL = 8


def passed_along(array, axis, by):
    size = lax.axis_size(axis)
    return lax.ppermute(array, axis, [(i, (i + by) % size) for i in range(size)])


def attend(q_rows, k_rows, v_rows, pattern_rows):
    token_count, head_count, head_dim = q_rows.shape
    block_count = token_count // BLOCK
    key_blocks = k_rows.reshape(block_count, BLOCK, head_dim)
    value_blocks = v_rows.reshape(block_count, BLOCK, head_dim)
    query_blocks = q_rows.reshape(block_count // 4, 4, BLOCK, head_count, head_dim)
    chosen_blocks = pattern_rows.reshape(block_count // 4, 4, NSEL)
    own_blocks = jnp.arange(block_count, dtype=jnp.int32).reshape(block_count // 4, 4)
    scaling = 1.0 / math.sqrt(head_dim)
    causal = jnp.arange(BLOCK)[:, None] >= jnp.arange(BLOCK)[None, :]

    def one_group(operands):
        q_group, chosen_group, own_group = operands
        is_live = chosen_group >= 0
        clamped = jnp.maximum(chosen_group, 0)
        key_sel = key_blocks[clamped]
        value_sel = value_blocks[clamped]
        scores = (
            jnp.einsum("qthd,qskd->qhtsk", q_group, key_sel, preferred_element_type=jnp.float32)
            * scaling
        )
        on_diagonal = clamped == own_group[:, None]
        allowed = is_live[:, None, None, :, None] & (
            jnp.logical_not(on_diagonal)[:, None, None, :, None] | causal[None, None, :, None, :]
        )
        scores = jnp.where(allowed, scores, -1e30)
        row_max = jnp.max(scores, axis=(3, 4), keepdims=True)
        weights = jnp.exp(scores - row_max)
        row_total = jnp.sum(weights, axis=(3, 4), keepdims=True)
        probability = (weights / row_total).astype(jnp.bfloat16)
        mixed_rows = jnp.einsum(
            "qhtsk,qskd->qthd", probability, value_sel, preferred_element_type=jnp.float32
        )
        return mixed_rows.astype(jnp.bfloat16)

    gathered_out = lax.map(one_group, (query_blocks, chosen_blocks, own_blocks))
    return gathered_out.reshape(token_count, head_count * head_dim)


def spread(rows_in, copies):
    leading = rows_in.shape[:-1]
    pieces = rows_in.reshape(leading + (HK, 1, HD))
    pieces = jnp.broadcast_to(pieces, leading + (HK, copies, HD))
    return pieces.reshape(leading + (HK * copies * HD,))


def local(residual, query_rows, key_rows, value_rows, pattern):
    carried = passed_along(residual, "segment", 1)
    seq_width = lax.axis_size("seq")
    heads_here = HQ // seq_width
    copies = seq_width // HK
    tokens_all = residual.shape[1] * seq_width
    kv_head = lax.axis_index("seq") * heads_here // (HQ // HK)
    chosen = lax.dynamic_index_in_dim(pattern[0], kv_head, axis=1, keepdims=False)
    own_queries = query_rows[0]
    key_copies = spread(key_rows[0], copies)
    value_copies = spread(value_rows[0], copies)
    moved_rows = [
        (
            lax.all_to_all(own_queries[layer_no], "seq", split_axis=1, concat_axis=0, tiled=True),
            lax.all_to_all(key_copies[layer_no], "seq", split_axis=1, concat_axis=0, tiled=True),
            lax.all_to_all(value_copies[layer_no], "seq", split_axis=1, concat_axis=0, tiled=True),
        )
        for layer_no in range(LAYERS)
    ]
    results = []
    for layer_no in range(LAYERS):
        q_here, k_here, v_here = moved_rows[layer_no]
        results.append(
            attend(q_here.reshape(tokens_all, heads_here, HD), k_here, v_here, chosen[layer_no])
        )
    layer_total = jnp.zeros((residual.shape[1], HQ * HD), jnp.float32)
    for layer_no in range(LAYERS):
        layer_total = layer_total + lax.all_to_all(
            results[layer_no], "seq", split_axis=0, concat_axis=1, tiled=True
        ).astype(jnp.float32)
    layer_sum = layer_total.astype(jnp.bfloat16)
    section_sum = carried[0].astype(jnp.float32) + layer_sum.astype(jnp.float32)
    return section_sum[None]


def solution(mesh):
    return jax.shard_map(
        local,
        mesh=mesh,
        in_specs=(
            P("segment", "seq", None),
            P("segment", None, "seq", None),
            P("segment", None, "seq", None),
            P("segment", None, "seq", None),
            P("segment", None, None, None, None),
        ),
        out_specs=P("segment", "seq", None),
        check_vma=False,
    )
```

profile of v0, /device:TPU:0, one launch (start us, length us, event | category | flops | bytes accessed | tf_op | source)
XLA Modules:
  0.0 313.8 jit_solution(8102645362013846129)
XLA Ops:
  0.0 1.1 fusion.33
  1.1 0.8 copy.90
  1.9 7.3 %all-to-all-start = ((bf16[128,8,128]{0,2,1:T(8,128)(2,1)}), bf16[128,8,128]{0,2,1:T(8,128)(2,1)S(1)}, u32[]{:S(2)}, u32[]{:S(2)}) async-start(bf16[128,8,128]{0,2,1:T(8,128)(2,1)} %bitcast.1), calls=%async_computation | async-start | bytes 524288 | tf_op jit(solution)/shard_map/all_to_all | solution.py:82
  9.2 1.1 fusion.32
  10.2 0.8 copy.91
  11.1 7.0 %all-to-all-done = bf16[128,8,128]{0,2,1:T(8,128)(2,1)S(1)} async-done(((bf16[128,8,128]{0,2,1:T(8,128)(2,1)}), bf16[128,8,128]{0,2,1:T(8,128)(2,1)S(1)}, u32[]{:S(2)}, u32[]{:S(2)}) %all-to-all-start) | async-done | bytes 262176 | tf_op jit(solution)/shard_map/all_to_all | solution.py:82
  18.1 3.6 %all-to-all-start.1 = ((bf16[128,8,128]{0,2,1:T(8,128)(2,1)}), bf16[128,8,128]{0,2,1:T(8,128)(2,1)S(1)}, u32[]{:S(2)}, u32[]{:S(2)}) async-start(bf16[128,8,128]{0,2,1:T(8,128)(2,1)} %bitcast.3), calls=%async_computation.1 | async-start | bytes 524288 | tf_op jit(solution)/shard_map/all_to_all | solution.py:81
  21.7 0.8 copy.92
  22.5 7.7 %all-to-all-done.1 = bf16[128,8,128]{0,2,1:T(8,128)(2,1)S(1)} async-done(((bf16[128,8,128]{0,2,1:T(8,128)(2,1)}), bf16[128,8,128]{0,2,1:T(8,128)(2,1)S(1)}, u32[]{:S(2)}, u32[]{:S(2)}) %all-to-all-start.1) | async-done | bytes 262176 | tf_op jit(solution)/shard_map/all_to_all | solution.py:81
  30.2 3.6 %all-to-all-start.4 = ((bf16[128,8,128]{0,2,1:T(8,128)(2,1)}), bf16[128,8,128]{0,2,1:T(8,128)(2,1)S(1)}, u32[]{:S(2)}, u32[]{:S(2)}) async-start(bf16[128,8,128]{0,2,1:T(8,128)(2,1)} %bitcast.10), calls=%async_computation.4 | async-start | bytes 524288 | tf_op jit(solution)/shard_map/all_to_all | solution.py:82
  33.8 0.8 copy.93
  34.7 7.7 %all-to-all-done.4 = bf16[128,8,128]{0,2,1:T(8,128)(2,1)S(1)} async-done(((bf16[128,8,128]{0,2,1:T(8,128)(2,1)}), bf16[128,8,128]{0,2,1:T(8,128)(2,1)S(1)}, u32[]{:S(2)}, u32[]{:S(2)}) %all-to-all-start.4) | async-done | bytes 262176 | tf_op jit(solution)/shard_map/all_to_all | solution.py:82
  42.4 3.5 %all-to-all-start.5 = ((bf16[128,8,128]{0,2,1:T(8,128)(2,1)}), bf16[128,8,128]{0,2,1:T(8,128)(2,1)S(1)}, u32[]{:S(2)}, u32[]{:S(2)}) async-start(bf16[128,8,128]{0,2,1:T(8,128)(2,1)} %bitcast.12), calls=%async_computation.5 | async-start | bytes 524288 | tf_op jit(solution)/shard_map/all_to_all | solution.py:81
  45.8 3.9 %fusion.31 = (bf16[1,1,128,8192]{3,2,1,0:T(8,128)(2,1)}, bf16[1,1,128,8192]{3,2,1,0:T(8,128)(2,1)S(1)}) fusion(bf16[1,2,128,8192]{3,2,1,0:T(8,128)(2,1)} %param.10), kind=kLoop, calls=%fused_computation.60 | loop fusion | bytes 8388608 | tf_op jit(solution)/shard_map/slice | solution.py:80
  49.7 4.1 %copy.55 = bf16[1,1,128,8192]{2,3,1,0:T(8,128)(2,1)} copy(bf16[1,1,128,8192]{3,2,1,0:T(8,128)(2,1)} %get-tuple-element.201) | data formatting | bytes 4194304 | tf_op jit(solution)/shard_map/slice | solution.py:80
  53.8 0.5 all-to-all-done.5
  54.4 5.5 %all-to-all-start.2 = ((bf16[128,8,1024]{0,2,1:T(8,128)(2,1)}), bf16[128,8,1024]{0,2,1:T(8,128)(2,1)}, u32[]{:S(2)}, u32[]{:S(2)}) async-start(bf16[128,8,1024]{0,2,1:T(8,128)(2,1)} %bitcast.5), calls=%async_computation.2 | async-start | bytes 4194304 | tf_op jit(solution)/shard_map/all_to_all | solution.py:80
  59.8 2.5 copy.63
  62.3 1.3 constant_dynamic-slice_fusion.2
  63.6 0.2 copy.56
  63.8 0.2 copy.57
  64.0 0.9 copy.64
  64.8 0.9 copy.65
  65.7 41.4 %all-to-all-done.2 = bf16[128,8,1024]{0,2,1:T(8,128)(2,1)} async-done(((bf16[128,8,1024]{0,2,1:T(8,128)(2,1)}), bf16[128,8,1024]{0,2,1:T(8,128)(2,1)}, u32[]{:S(2)}, u32[]{:S(2)}) %all-to-all-start.2) | async-done | bytes 2097184 | tf_op jit(solution)/shard_map/all_to_all | solution.py:80
  107.1 4.5 %all-to-all-start.6 = ((bf16[128,8,1024]{0,2,1:T(8,128)(2,1)}), bf16[128,8,1024]{0,2,1:T(8,128)(2,1)}, u32[]{:S(2)}, u32[]{:S(2)}) async-start(bf16[128,8,1024]{0,2,1:T(8,128)(2,1)} %bitcast.14), calls=%async_computation.6 | async-start | bytes 4194304 | tf_op jit(solution)/shard_map/all_to_all | solution.py:80
  111.7 1.8 broadcast.127.clone.1
  113.5 58.7 %while.22 = (s32[]{:T(128)}, bf16[2,4,128,8,128]{2,4,3,1,0:T(8,128)(2,1)}, s32[2,4,8]{2,1,0:T(4,128)S(1)}, bf16[8,128,128]{2,1,0:T(8,128)(2,1)S(1)}, s32[2,4]{1,...) while((s32[]{:T(128)}, ...), condition=%wide.region_3.4_spmd.clone, body=%wide.region_0.3_spmd.clone.sunk | while | flops 2199397376 | bytes 60938512 | solution.py:56
  113.6 0.5 or_and_fusion.4
  114.2 0.7 gather_fusion.1
  114.9 8.4 %fusion.56 = (f32[4,8,128]{2,1,0:T(8,128)S(1)}, f32[4,8,128,128,8]{3,2,4,1,0:T(8,128)}) fusion(pred[4,128,8,128]{1,3,2,0:T(8,128)(4,1)S(1)} %or_and_fusion.4, bf16[4,8,128,128,1]{3,2,4,1,0:T(8,128)(2,1)S(1)} %bitcast.199, bf16[2,4,128,8,128]{2,4,3,1,0:T(8,128)(2,1)} %get-tuple-element.357, s32[]{:T(128)} %get-tuple-element.343), kind=kOutput, calls=%fused_computation.10.clone.1 | convolution fusion | flops 1086320640 | bytes 19415552 | tf_op jit(solution)/shard_map/while/body/eval_jaxpr/qthd,qskd->qhtsk/dot_general | solution.py:39
  123.3 9.5 %fusion.57 = f32[4,8,128]{2,1,0:T(8,128)S(1)} fusion(f32[4,8,128,128,8]{3,2,4,1,0:T(8,128)} %get-tuple-element.298, f32[4,8,128]{2,1,0:T(8,128)S(1)} %get-tuple-element.299, pred[4,128,8,128]{1,3,2,0:T(8,128)(4,1)S(1)} %or_and_fusion.4), kind=kLoop, calls=%fused_computation.9.clone.1 | loop fusion | flops 16773120 | bytes 17334272 | tf_op jit(solution)/shard_map/while/body/eval_jaxpr/reduce_sum | solution.py:49
  132.8 0.7 gather_fusion
  133.6 9.3 %fusion.58 = bf16[2,4,128,8,128]{2,4,3,1,0:T(8,128)(2,1)} fusion(bf16[2,4,128,8,128]{2,4,3,1,0:T(8,128)(2,1)} %get-tuple-element.344, s32[]{:T(128)} %get-tuple-element.343, bf16[4,8,128,128,1]{3,2,4,1,0:T(8,128)(2,1)S(1)} %bitcast.201, f32[4,8,128,128,8]{3,2,4,1,0:T(8,128)} %get-tuple-element.298, f32[4,8,128]{2,1,0:T(8,128)S(1)} %fusion.57, ...), kind=kOutput, calls=%fused_computation.15.clone.1 | convolution fusion | flops 1095237632 | bytes 19431936 | tf_op jit(solution)/shard_map/while/body/eval_jaxpr/qhtsk,qskd->qthd/dot_general | solution.py:51
  142.9 0.5 or_and_fusion.4
  143.5 0.7 gather_fusion.1
  144.3 8.4 %fusion.56 = (f32[4,8,128]{2,1,0:T(8,128)S(1)}, f32[4,8,128,128,8]{3,2,4,1,0:T(8,128)}) fusion(pred[4,128,8,128]{1,3,2,0:T(8,128)(4,1)S(1)} %or_and_fusion.4, bf16[4,8,128,128,1]{3,2,4,1,0:T(8,128)(2,1)S(1)} %bitcast.199, bf16[2,4,128,8,128]{2,4,3,1,0:T(8,128)(2,1)} %get-tuple-element.357, s32[]{:T(128)} %get-tuple-element.343), kind=kOutput, calls=%fused_computation.10.clone.1 | convolution fusion | flops 1086320640 | bytes 19415552 | tf_op jit(solution)/shard_map/while/body/eval_jaxpr/qthd,qskd->qhtsk/dot_general | solution.py:39
  152.6 9.5 %fusion.57 = f32[4,8,128]{2,1,0:T(8,128)S(1)} fusion(f32[4,8,128,128,8]{3,2,4,1,0:T(8,128)} %get-tuple-element.298, f32[4,8,128]{2,1,0:T(8,128)S(1)} %get-tuple-element.299, pred[4,128,8,128]{1,3,2,0:T(8,128)(4,1)S(1)} %or_and_fusion.4), kind=kLoop, calls=%fused_computation.9.clone.1 | loop fusion | flops 16773120 | bytes 17334272 | tf_op jit(solution)/shard_map/while/body/eval_jaxpr/reduce_sum | solution.py:49
  162.2 0.7 gather_fusion
  162.9 9.3 %fusion.58 = bf16[2,4,128,8,128]{2,4,3,1,0:T(8,128)(2,1)} fusion(bf16[2,4,128,8,128]{2,4,3,1,0:T(8,128)(2,1)} %get-tuple-element.344, s32[]{:T(128)} %get-tuple-element.343, bf16[4,8,128,128,1]{3,2,4,1,0:T(8,128)(2,1)S(1)} %bitcast.201, f32[4,8,128,128,8]{3,2,4,1,0:T(8,128)} %get-tuple-element.298, f32[4,8,128]{2,1,0:T(8,128)S(1)} %fusion.57, ...), kind=kOutput, calls=%fused_computation.15.clone.1 | convolution fusion | flops 1095237632 | bytes 19431936 | tf_op jit(solution)/shard_map/while/body/eval_jaxpr/qhtsk,qskd->qthd/dot_general | solution.py:51
  172.2 3.9 %copy.80 = bf16[8,128,1024]{2,1,0:T(8,128)(2,1)} copy(bf16[8,128,1024]{1,2,0:T(8,128)(2,1)} %bitcast.205) | data formatting | bytes 4194304 | tf_op jit(solution)/shard_map/all_to_all | solution.py:94
  176.1 5.9 %all-to-all-start.3 = ((bf16[8,128,1024]{2,1,0:T(8,128)(2,1)}), bf16[8,128,1024]{2,1,0:T(8,128)(2,1)}, u32[]{:S(2)}, u32[]{:S(2)}) async-start(bf16[8,128,1024]{2,1,0:T(8,128)(2,1)} %copy.80), calls=%async_computation.3 | async-start | bytes 4194304 | tf_op jit(solution)/shard_map/all_to_all | solution.py:94
  182.0 1.8 broadcast.127.clone
  183.8 58.7 %while.23 = (s32[]{:T(128)}, bf16[2,4,128,8,128]{2,4,3,1,0:T(8,128)(2,1)}, s32[2,4,8]{2,1,0:T(4,128)S(1)}, bf16[8,128,128]{2,1,0:T(8,128)(2,1)S(1)}, s32[2,4]{1,...) while((s32[]{:T(128)}, ...), condition=%wide.region_7.8_spmd.clone, body=%wide.region_4.7_spmd.clone.sunk | while | flops 2199397376 | bytes 60938512 | solution.py:56
  184.0 0.5 or_and_fusion.5
  184.5 0.7 gather_fusion.3
  185.3 8.4 %fusion.63 = (f32[4,8,128]{2,1,0:T(8,128)S(1)}, f32[4,8,128,128,8]{3,2,4,1,0:T(8,128)}) fusion(pred[4,128,8,128]{1,3,2,0:T(8,128)(4,1)S(1)} %or_and_fusion.5, bf16[4,8,128,128,1]{3,2,4,1,0:T(8,128)(2,1)S(1)} %bitcast.200, bf16[2,4,128,8,128]{2,4,3,1,0:T(8,128)(2,1)} %get-tuple-element.333, s32[]{:T(128)} %get-tuple-element.319), kind=kOutput, calls=%fused_computation.34.clone.1 | convolution fusion | flops 1086320640 | bytes 19415552 | tf_op jit(solution)/shard_map/while/body/eval_jaxpr/qthd,qskd->qhtsk/dot_general | solution.py:39
  193.7 9.5 %fusion.64 = f32[4,8,128]{2,1,0:T(8,128)S(1)} fusion(f32[4,8,128,128,8]{3,2,4,1,0:T(8,128)} %get-tuple-element.309, f32[4,8,128]{2,1,0:T(8,128)S(1)} %get-tuple-element.310, pred[4,128,8,128]{1,3,2,0:T(8,128)(4,1)S(1)} %or_and_fusion.5), kind=kLoop, calls=%fused_computation.33.clone.1 | loop fusion | flops 16773120 | bytes 17334272 | tf_op jit(solution)/shard_map/while/body/eval_jaxpr/reduce_sum | solution.py:49
  203.2 0.7 gather_fusion.2
  203.9 9.3 %fusion.65 = bf16[2,4,128,8,128]{2,4,3,1,0:T(8,128)(2,1)} fusion(bf16[2,4,128,8,128]{2,4,3,1,0:T(8,128)(2,1)} %get-tuple-element.320, s32[]{:T(128)} %get-tuple-element.319, bf16[4,8,128,128,1]{3,2,4,1,0:T(8,128)(2,1)S(1)} %bitcast.202, f32[4,8,128,128,8]{3,2,4,1,0:T(8,128)} %get-tuple-element.309, f32[4,8,128]{2,1,0:T(8,128)S(1)} %fusion.64, ...), kind=kOutput, calls=%fused_computation.39.clone.1 | convolution fusion | flops 1095237632 | bytes 19431936 | tf_op jit(solution)/shard_map/while/body/eval_jaxpr/qhtsk,qskd->qthd/dot_general | solution.py:51
  213.3 0.5 or_and_fusion.5
  213.9 0.7 gather_fusion.3
  214.6 8.4 %fusion.63 = (f32[4,8,128]{2,1,0:T(8,128)S(1)}, f32[4,8,128,128,8]{3,2,4,1,0:T(8,128)}) fusion(pred[4,128,8,128]{1,3,2,0:T(8,128)(4,1)S(1)} %or_and_fusion.5, bf16[4,8,128,128,1]{3,2,4,1,0:T(8,128)(2,1)S(1)} %bitcast.200, bf16[2,4,128,8,128]{2,4,3,1,0:T(8,128)(2,1)} %get-tuple-element.333, s32[]{:T(128)} %get-tuple-element.319), kind=kOutput, calls=%fused_computation.34.clone.1 | convolution fusion | flops 1086320640 | bytes 19415552 | tf_op jit(solution)/shard_map/while/body/eval_jaxpr/qthd,qskd->qhtsk/dot_general | solution.py:39
  223.0 9.5 %fusion.64 = f32[4,8,128]{2,1,0:T(8,128)S(1)} fusion(f32[4,8,128,128,8]{3,2,4,1,0:T(8,128)} %get-tuple-element.309, f32[4,8,128]{2,1,0:T(8,128)S(1)} %get-tuple-element.310, pred[4,128,8,128]{1,3,2,0:T(8,128)(4,1)S(1)} %or_and_fusion.5), kind=kLoop, calls=%fused_computation.33.clone.1 | loop fusion | flops 16773120 | bytes 17334272 | tf_op jit(solution)/shard_map/while/body/eval_jaxpr/reduce_sum | solution.py:49
  232.5 0.7 gather_fusion.2
  233.3 9.3 %fusion.65 = bf16[2,4,128,8,128]{2,4,3,1,0:T(8,128)(2,1)} fusion(bf16[2,4,128,8,128]{2,4,3,1,0:T(8,128)(2,1)} %get-tuple-element.320, s32[]{:T(128)} %get-tuple-element.319, bf16[4,8,128,128,1]{3,2,4,1,0:T(8,128)(2,1)S(1)} %bitcast.202, f32[4,8,128,128,8]{3,2,4,1,0:T(8,128)} %get-tuple-element.309, f32[4,8,128]{2,1,0:T(8,128)S(1)} %fusion.64, ...), kind=kOutput, calls=%fused_computation.39.clone.1 | convolution fusion | flops 1095237632 | bytes 19431936 | tf_op jit(solution)/shard_map/while/body/eval_jaxpr/qhtsk,qskd->qthd/dot_general | solution.py:51
  242.5 3.9 %copy.81 = bf16[8,128,1024]{2,1,0:T(8,128)(2,1)} copy(bf16[8,128,1024]{1,2,0:T(8,128)(2,1)} %bitcast.204) | data formatting | bytes 4194304 | tf_op jit(solution)/shard_map/all_to_all | solution.py:94
  246.5 6.0 %all-to-all-start.7 = ((bf16[8,128,1024]{2,1,0:T(8,128)(2,1)}), bf16[8,128,1024]{2,1,0:T(8,128)(2,1)S(1)}, u32[]{:S(2)}, u32[]{:S(2)}) async-start(bf16[8,128,1024]{2,1,0:T(8,128)(2,1)} %copy.81), calls=%async_computation.7 | async-start | bytes 4194304 | tf_op jit(solution)/shard_map/all_to_all | solution.py:94
  252.5 4.1 %copy.52 = bf16[1,128,8192]{1,2,0:T(8,128)(2,1)} copy(bf16[1,128,8192]{2,1,0:T(8,128)(2,1)} %param.9) | data formatting | bytes 4194304 | tf_op args[0]
  256.5 3.9 %copy.60 = bf16[8,128,1024]{1,2,0:T(8,128)(2,1)} copy(bf16[8,128,1024]{2,1,0:T(8,128)(2,1)} %all-to-all-done.3) | data formatting | bytes 4194304 | tf_op jit(solution)/shard_map/all_to_all | solution.py:94
  260.5 38.8 %all-to-all-done.7 = bf16[8,128,1024]{2,1,0:T(8,128)(2,1)S(1)} async-done(((bf16[8,128,1024]{2,1,0:T(8,128)(2,1)}), bf16[8,128,1024]{2,1,0:T(8,128)(2,1)S(1)}, u32[]{:S(2)}, u32[]{:S(2)}) %all-to-all-start.7) | async-done | bytes 2097184 | tf_op jit(solution)/shard_map/all_to_all | solution.py:94
  299.2 2.4 copy.68
  301.6 2.6 fusion.30
  304.3 4.0 %bitcast_add_fusion = f32[1,128,8192]{1,2,0:T(8,128)} fusion(bf16[1,128,8192]{1,2,0:T(8,128)(2,1)} %collective-permute-done, f32[1,128,8192]{1,2,0:T(8,128)S(1)} %bitcast.203), kind=kLoop, calls=%fused_computation.54 | loop fusion | flops 2097152 | bytes 10485760 | tf_op jit(solution)/shard_map/add | solution.py:98
  308.2 5.6 %copy.69 = f32[1,128,8192]{2,1,0:T(8,128)} copy(f32[1,128,8192]{1,2,0:T(8,128)} %bitcast_add_fusion) | data formatting | bytes 8388608 | tf_op jit(solution)/shard_map/add | solution.py:98
  (35 shorter events, 0.8 us)
Async XLA Ops:
  1.9 16.2 %all-to-all-start = ((bf16[128,8,128]{0,2,1:T(8,128)(2,1)}), bf16[128,8,128]{0,2,1:T(8,128)(2,1)S(1)}, u32[]{:S(2)}, u32[]{:S(2)}) async-start(bf16[128,8,128]{0,2,1:T(8,128)(2,1)} %bitcast.1), calls=%async_computation | async-start | bytes 524288 | tf_op jit(solution)/shard_map/all_to_all | solution.py:82
  18.1 12.2 %all-to-all-start.1 = ((bf16[128,8,128]{0,2,1:T(8,128)(2,1)}), bf16[128,8,128]{0,2,1:T(8,128)(2,1)S(1)}, u32[]{:S(2)}, u32[]{:S(2)}) async-start(bf16[128,8,128]{0,2,1:T(8,128)(2,1)} %bitcast.3), calls=%async_computation.1 | async-start | bytes 524288 | tf_op jit(solution)/shard_map/all_to_all | solution.py:81
  30.2 12.1 %all-to-all-start.4 = ((bf16[128,8,128]{0,2,1:T(8,128)(2,1)}), bf16[128,8,128]{0,2,1:T(8,128)(2,1)S(1)}, u32[]{:S(2)}, u32[]{:S(2)}) async-start(bf16[128,8,128]{0,2,1:T(8,128)(2,1)} %bitcast.10), calls=%async_computation.4 | async-start | bytes 524288 | tf_op jit(solution)/shard_map/all_to_all | solution.py:82
  42.4 12.0 %all-to-all-start.5 = ((bf16[128,8,128]{0,2,1:T(8,128)(2,1)}), bf16[128,8,128]{0,2,1:T(8,128)(2,1)S(1)}, u32[]{:S(2)}, u32[]{:S(2)}) async-start(bf16[128,8,128]{0,2,1:T(8,128)(2,1)} %bitcast.12), calls=%async_computation.5 | async-start | bytes 524288 | tf_op jit(solution)/shard_map/all_to_all | solution.py:81
  54.4 52.8 %all-to-all-start.2 = ((bf16[128,8,1024]{0,2,1:T(8,128)(2,1)}), bf16[128,8,1024]{0,2,1:T(8,128)(2,1)}, u32[]{:S(2)}, u32[]{:S(2)}) async-start(bf16[128,8,1024]{0,2,1:T(8,128)(2,1)} %bitcast.5), calls=%async_computation.2 | async-start | bytes 4194304 | tf_op jit(solution)/shard_map/all_to_all | solution.py:80
  107.1 69.0 %all-to-all-start.6 = ((bf16[128,8,1024]{0,2,1:T(8,128)(2,1)}), bf16[128,8,1024]{0,2,1:T(8,128)(2,1)}, u32[]{:S(2)}, u32[]{:S(2)}) async-start(bf16[128,8,1024]{0,2,1:T(8,128)(2,1)} %bitcast.14), calls=%async_computation.6 | async-start | bytes 4194304 | tf_op jit(solution)/shard_map/all_to_all | solution.py:80
  176.1 7.7 %copy-start = (bf16[8,128,128]{2,1,0:T(8,128)(2,1)S(1)}, bf16[8,128,128]{2,1,0:T(8,128)(2,1)}, u32[]{:S(2)}) copy-start(bf16[8,128,128]{2,1,0:T(8,128)(2,1)} %copy.64) | copy-start | bytes 786436
  176.1 7.7 %copy-start.1 = (bf16[8,128,128]{2,1,0:T(8,128)(2,1)S(1)}, bf16[8,128,128]{2,1,0:T(8,128)(2,1)}, u32[]{:S(2)}) copy-start(bf16[8,128,128]{2,1,0:T(8,128)(2,1)} %copy.65) | copy-start | bytes 786436
  176.1 7.7 %copy-start.2 = (s32[1,1,1,8,8]{4,3,2,1,0:T(8,128)S(1)}, s32[1,1,1,8,8]{4,3,2,1,0:T(8,128)}, u32[]{:S(2)}) copy-start(s32[1,1,1,8,8]{4,3,2,1,0:T(8,128)} %get-tuple-element.208) | copy-start | bytes 772
  176.1 70.4 %all-to-all-start.3 = ((bf16[8,128,1024]{2,1,0:T(8,128)(2,1)}), bf16[8,128,1024]{2,1,0:T(8,128)(2,1)}, u32[]{:S(2)}, u32[]{:S(2)}) async-start(bf16[8,128,1024]{2,1,0:T(8,128)(2,1)} %copy.80), calls=%async_computation.3 | async-start | bytes 4194304 | tf_op jit(solution)/shard_map/all_to_all | solution.py:94
  246.5 52.7 %all-to-all-start.7 = ((bf16[8,128,1024]{2,1,0:T(8,128)(2,1)}), bf16[8,128,1024]{2,1,0:T(8,128)(2,1)S(1)}, u32[]{:S(2)}, u32[]{:S(2)}) async-start(bf16[8,128,1024]{2,1,0:T(8,128)(2,1)} %copy.81), calls=%async_computation.7 | async-start | bytes 4194304 | tf_op jit(solution)/shard_map/all_to_all | solution.py:94
  256.5 47.7 %collective-permute-start = (bf16[1,128,8192]{1,2,0:T(8,128)(2,1)}, bf16[1,128,8192]{1,2,0:T(8,128)(2,1)}, u32[]{:S(2)}, u32[]{:S(2)}) collective-permute-start(bf16[1,128,8192]{1,2,0:T(8,128)(2,1)} %copy.52), channel_id=1, source_target_pairs={{0,8},{8,16},{16,24},{24,0},{1,9},{9,17},{17,25},{25,1},{2,10},{10... | collective-permute-start | bytes 6291464 | tf_op jit(solution)/shard_map/ppermute | solution.py:18
where the time goes:
time: 315 us; the launch traced here: 314 us
  waiting for transfers between devices  103 us (33%)
  matrix products  70.6 us (22%)
  local copies, waits for them, and re-layouts  53.1 us (17%)
  other arithmetic  46.9 us (15%)
  starting transfers between devices  39.8 us (13%)
    all_to_all x2, waiting for transfers between devices, local(): lax.all_to_all(own_queries[layer_no], 'seq', split_axis=1, concat_axis=0,...  41.4 us
    all_to_all x2, waiting for transfers between devices, local(): lax.all_to_all(results[layer_no], 'seq', split_axis=0, concat_axis=1, til...  38.8 us
    reduce_sum x4, other arithmetic, one_group(): row_total = jnp.sum(weights, axis=(3, 4), keepdims=True)  38.1 us
    dot_general x4, matrix products, one_group(): jnp.einsum('qhtsk,qskd->qthd', probability, value_sel, preferred_element_...  37.1 us
    dot_general x4, matrix products, one_group(): jnp.einsum('qthd,qskd->qhtsk', q_group, key_sel, preferred_element_type=j...  33.5 us
    all_to_all x2, waiting for transfers between devices, local(): lax.all_to_all(value_copies[layer_no], 'seq', split_axis=1, concat_axis=0...  14.7 us
    all_to_all x4, local copies, waits for them, and re-layouts, local(): lax.all_to_all(results[layer_no], 'seq', split_axis=0, concat_axis=1, til...  14.2 us
    all_to_all x2, starting transfers between devices, local(): lax.all_to_all(results[layer_no], 'seq', split_axis=0, concat_axis=1, til...  11.9 us
  transfers between devices with their start and end apart: 9, of which 6 were waited for; matrix products, arithmetic and copies ran while one was open for 51% of the time, Pallas kernels for 0%

commit v1 on v0

v1 whole, which is shorter than its diff:
```python
import functools
import math

import jax
import jax.numpy as jnp
from jax import lax
from jax.experimental import pallas as pl
from jax.experimental.pallas import tpu as pltpu
from jax.sharding import PartitionSpec as P

HQ = 64
HK = 8
HD = 128
CHUNKS = (2, 2, 2, 2)


def columns_of(ring):
    width = 1
    while 2 * (2 * width) ** 2 <= ring:
        width *= 2
    return width


def rotated(array, axis, move):
    size = lax.axis_size(axis)
    return lax.ppermute(array, axis, [(i, move(i)) for i in range(size)])


def collected(block, width):
    ring = lax.axis_size("seq")
    up = lambda i: (i + width) % ring
    found = []
    held = block
    for step in range(ring // width):
        if step:
            held = rotated(held, "seq", up)
        found.append(held)
        for by in range(1, width):
            across = lambda i, by=by: i // width * width + (i + by) % width
            found.append(rotated(held, "seq", across))
    return found


def attend_body(layers, first_head, live_ref, q_ref, *refs):
    kv_refs, (carried_ref, _, out_ref) = refs[:-3], refs[-3:]
    tokens = q_ref.shape[1]
    group = pl.program_id(0)
    factor = math.log2(math.e) / math.sqrt(HD)
    row = lax.broadcasted_iota(jnp.int32, (tokens, tokens), 0)
    col = lax.broadcasted_iota(jnp.int32, (tokens, tokens), 1)
    causal = row >= col
    ones = jnp.ones((tokens, HD), jnp.bfloat16)
    for layer in range(layers):
        own = kv_refs[0]
        visible_key = jnp.broadcast_to(own[layer, 0:1, :], (tokens, HD))
        keys, values, weights = [own[layer]], [own[layers + layer]], [ones]
        for place in range(1, len(kv_refs)):
            live = live_ref[layer, first_head + group, place] > 0
            keys.append(jnp.where(live, kv_refs[place][layer], visible_key))
            values.append(jnp.where(live, kv_refs[place][layers + layer], jnp.zeros_like(ones)))
            weights.append(jnp.where(live, ones, jnp.zeros_like(ones)))
        keys = jnp.concatenate(keys, axis=0)
        values = jnp.concatenate(
            [jnp.concatenate(values, axis=0), jnp.concatenate(weights, axis=0)], axis=1
        )
        for head in range(q_ref.shape[2] // HD):
            lanes = slice(head * HD, (head + 1) * HD)
            scores = lax.dot_general(
                q_ref[layer, :, lanes],
                keys,
                (((1,), (1,)), ((), ())),
                preferred_element_type=jnp.float32,
            )
            own_scores = jnp.where(causal, scores[:, :tokens], -1e30)
            scores = jnp.concatenate([own_scores, scores[:, tokens:]], axis=1)
            row_max = jnp.max(scores, axis=1, keepdims=True)
            weight = jnp.exp2((scores - row_max) * factor).astype(jnp.bfloat16)
            mixed = jnp.dot(weight, values, preferred_element_type=jnp.float32)
            attended = mixed[:, :HD] / mixed[:, HD:]
            total = attended.astype(jnp.bfloat16).astype(jnp.float32)
            if layer:
                total = out_ref[:, lanes] + total
            if layer == layers - 1:
                total = total.astype(jnp.bfloat16).astype(jnp.float32)
                total = carried_ref[:, lanes].astype(jnp.float32) + total
            out_ref[:, lanes] = total


def attend(live, queries, blocks, carried, out, first_head):
    layers, tokens, width = queries.shape
    heads = blocks[0].shape[2] // HD
    lanes = width // HK
    operands = [live, queries, *blocks, carried]
    whole = pl.BlockSpec(memory_space=pl.ANY)
    aliases = {}
    if out is None:
        out = carried
    else:
        aliases = {len(operands): 0}
    return pl.pallas_call(
        functools.partial(attend_body, layers, first_head),
        grid_spec=pltpu.PrefetchScalarGridSpec(
            num_scalar_prefetch=1,
            grid=(heads,),
            in_specs=[
                pl.BlockSpec((layers, tokens, lanes), lambda g, _: (0, 0, first_head + g)),
                *[pl.BlockSpec((2 * layers, tokens, HD), lambda g, _: (0, 0, g)) for _ in blocks],
                pl.BlockSpec((tokens, lanes), lambda g, _: (0, first_head + g)),
                whole,
            ],
            out_specs=pl.BlockSpec((tokens, lanes), lambda g, _: (0, first_head + g)),
        ),
        out_shape=jax.ShapeDtypeStruct((tokens, width), jnp.float32),
        input_output_aliases=aliases,
        compiler_params=pltpu.CompilerParams(vmem_limit_bytes=32 << 20),
        cost_estimate=pl.CostEstimate(
            flops=4 * layers * tokens * lanes * heads * tokens * len(blocks),
            bytes_accessed=heads * tokens * (layers * lanes * 2 + lanes * 6),
            transcendentals=layers * tokens * (lanes // HD) * heads * tokens * len(blocks),
        ),
    )(*operands, out)


def local(residual, query_rows, key_rows, value_rows, pattern):
    ring = lax.axis_size("seq")
    segments = lax.axis_size("segment")
    width = columns_of(ring)
    me = lax.axis_index("seq")
    carried = rotated(residual[0], "segment", lambda i: (i + 1) % segments)
    place = jnp.arange(ring, dtype=jnp.int32)
    rows_below, shift = place // width, place % width
    held_block = (me // width - rows_below) % (ring // width) * width + (me - shift) % width
    chosen = lax.dynamic_index_in_dim(pattern[0], me, axis=2, keepdims=False)
    live = jnp.any(chosen[:, :, :, None] == held_block, axis=2).astype(jnp.int32)
    out = None
    first_head = 0
    for heads in CHUNKS:
        lanes = slice(first_head * HD, (first_head + heads) * HD)
        block = jnp.concatenate([key_rows[0, :, :, lanes], value_rows[0, :, :, lanes]], axis=0)
        out = attend(live, query_rows[0], collected(block, width), carried, out, first_head)
        first_head += heads
    return out[None]


def solution(mesh):
    return jax.shard_map(
        local,
        mesh=mesh,
        in_specs=(
            P("segment", "seq", None),
            P("segment", None, "seq", None),
            P("segment", None, "seq", None),
            P("segment", None, "seq", None),
            P("segment", None, None, None, None),
        ),
        out_specs=P("segment", "seq", None),
        check_vma=False,
    )
```

time: 315 us -> 120 us (0.38)
  matrix products: 70.6 us -> 0 us
  waiting for transfers between devices: 103 us -> 42.8 us
  other arithmetic: 46.9 us -> 0.22 us
  local copies, waits for them, and re-layouts: 53.1 us -> 11.9 us
  Pallas kernels: 0 us -> 32.8 us
  starting transfers between devices: 39.8 us -> 31.3 us
    all_to_all x8 -> x0, waiting for transfers between devices: 103 us -> none  [the longest x2 41.4 us: local(): lax.all_to_all(own_queries[layer_no], 'seq', split_axis=1, concat_axis=0,...]
    dot_general x8 -> x0, matrix products: 70.6 us -> none  [the longest x4 37.1 us: one_group(): jnp.einsum('qhtsk,qskd->qthd', probability, value_sel, preferred_element_...]
    ppermute x1 -> x29, waiting for transfers between devices: 0.01 us -> 42.8 us  [rotated(): return lax.ppermute(array, axis, [(i, move(i)) for i in range(size)])]
    all_to_all x8 -> x0, starting transfers between devices: 39.8 us -> none  [the longest x2 11.9 us: local(): lax.all_to_all(results[layer_no], 'seq', split_axis=0, concat_axis=1, til...]
    reduce_sum x4 -> x0, other arithmetic: 38.1 us -> none  [one_group(): row_total = jnp.sum(weights, axis=(3, 4), keepdims=True)]
    pallas_call x0 -> x4, Pallas kernels: none -> 32.8 us  [attend(): pl.pallas_call(functools.partial(attend_body, layers, first_head), grid_s...]
    ppermute x1 -> x29, starting transfers between devices: 0.01 us -> 31.3 us  [rotated(): return lax.ppermute(array, axis, [(i, move(i)) for i in range(size)])]
    all_to_all x4 -> x0, local copies, waits for them, and re-layouts: 14.2 us -> none  [local(): lax.all_to_all(results[layer_no], 'seq', split_axis=0, concat_axis=1, til...]
  transfers between devices with their start and end apart: 9 -> 29, of which waited for: 6 -> 15; matrix products, arithmetic and copies ran while one was open for 51% -> 1% of each run, Pallas kernels for 0% -> 21%
where the time goes in v1:
time: 120 us; the launch traced here: 119 us
  waiting for transfers between devices  42.8 us (36%)
  Pallas kernels  32.8 us (27%)
  starting transfers between devices  31.3 us (26%)
  local copies, waits for them, and re-layouts  11.9 us (10%)
    ppermute x29, waiting for transfers between devices, rotated(): return lax.ppermute(array, axis, [(i, move(i)) for i in range(size)])  42.8 us
    pallas_call x4, Pallas kernels, attend(): pl.pallas_call(functools.partial(attend_body, layers, first_head), grid_s...  32.8 us
    ppermute x29, starting transfers between devices, rotated(): return lax.ppermute(array, axis, [(i, move(i)) for i in range(size)])  31.3 us
    unnamed x44, local copies, waits for them, and re-layouts  10.5 us
  transfers between devices with their start and end apart: 29, of which 15 were waited for; matrix products, arithmetic and copies ran while one was open for 1% of the time, Pallas kernels for 21%

profile of v1, /device:TPU:0, one launch (start us, length us, event | category | flops | bytes accessed | tf_op | source)
XLA Modules:
  0.0 119.2 jit_solution(457028889827972004)
XLA Ops:
  0.0 0.5 collective-permute-start.7
  0.5 1.4 %slice_bitcast_fusion = (bf16[2,128,256]{2,1,0:T(8,128)(2,1)S(1)}, bf16[2,128,256]{2,1,0:T(8,128)(2,1)S(1)}, bf16[2,128,256]{2,1,0:T(8,128)(2,1)S(1)}, bf16[2,12...) fusion(bf16[1,2,128,1024]{3,2,1,0:T(8,128)(2,1)} %param.8, ...), kind=kLoop, calls=%fused_computation.4 | loop fusion | bytes 2097152 | tf_op jit(solution)/shard_map/squeeze | solution.py:139
  1.9 2.7 %collective-permute-start.23 = (bf16[4,128,256]{2,1,0:T(8,128)(2,1)S(1)}, bf16[4,128,256]{2,1,0:T(8,128)(2,1)S(1)}, u32[]{:S(2)}, u32[]{:S(2)}) collective-permute-start(bf16[4,128,256]{2,1,0:T(8,128)(2,1)S(1)} %pad_maximum_fusion.3.refs_0_), channel_id=1, source_target_pairs={{0,2},{1,3},{2,4},{3,5},{4,6},{5,7},{6,0},{7,1},{8,10},{9,11},{10,... | collective-permute-start | bytes 786440 | tf_op jit(solution)/shard_map/ppermute | solution.py:26
  4.5 1.5 %collective-permute-start.22 = (bf16[4,128,256]{2,1,0:T(8,128)(2,1)S(1)}, bf16[4,128,256]{2,1,0:T(8,128)(2,1)S(1)}, u32[]{:S(2)}, u32[]{:S(2)}) collective-permute-start(bf16[4,128,256]{2,1,0:T(8,128)(2,1)S(1)} %pad_maximum_fusion.3.refs_0_), channel_id=1, source_target_pairs={{0,1},{1,0},{2,3},{3,2},{4,5},{5,4},{6,7},{7,6},{8,9},{9,8},{10,11... | collective-permute-start | bytes 786440 | tf_op jit(solution)/shard_map/ppermute | solution.py:26
  6.1 1.6 %collective-permute-start.16 = (bf16[4,128,256]{2,1,0:T(8,128)(2,1)S(1)}, bf16[4,128,256]{2,1,0:T(8,128)(2,1)S(1)}, u32[]{:S(2)}, u32[]{:S(2)}) collective-permute-start(bf16[4,128,256]{2,1,0:T(8,128)(2,1)S(1)} %pad_maximum_fusion.2.refs_0_), channel_id=1, source_target_pairs={{0,2},{1,3},{2,4},{3,5},{4,6},{5,7},{6,0},{7,1},{8,10},{9,11},{10,... | collective-permute-start | bytes 786440 | tf_op jit(solution)/shard_map/ppermute | solution.py:26
  7.7 0.5 collective-permute-start.15
  8.3 4.5 %collective-permute-done.23.refs_2_ = bf16[4,128,256]{2,1,0:T(8,128)(2,1)S(1)} collective-permute-done((bf16[4,128,256]{2,1,0:T(8,128)(2,1)S(1)}, bf16[4,128,256]{2,1,0:T(8,128)(2,1)S(1)}, u32[]{:S(2)}, u32[]{:S(2)}) %collective-permute-start.23) | collective-permute-done | bytes 262176 | tf_op jit(solution)/shard_map/ppermute | solution.py:26
  12.8 0.3 collective-permute-start.9
  13.1 0.3 collective-permute-done.22.refs_1_
  13.5 0.7 copy-done.2
  14.2 1.5 %collective-permute-start.8 = (bf16[4,128,256]{2,1,0:T(8,128)(2,1)S(1)}, bf16[4,128,256]{2,1,0:T(8,128)(2,1)S(1)}, u32[]{:S(2)}, u32[]{:S(2)}) collective-permute-start(bf16[4,128,256]{2,1,0:T(8,128)(2,1)S(1)} %pad_maximum_fusion.1.refs_0_), channel_id=1, source_target_pairs={{0,1},{1,0},{2,3},{3,2},{4,5},{5,4},{6,7},{7,6},{8,9},{9,8},{10,11... | collective-permute-start | bytes 786440 | tf_op jit(solution)/shard_map/ppermute | solution.py:26
  15.7 2.8 %collective-permute-done.16.refs_2_ = bf16[4,128,256]{2,1,0:T(8,128)(2,1)S(1)} collective-permute-done((bf16[4,128,256]{2,1,0:T(8,128)(2,1)S(1)}, bf16[4,128,256]{2,1,0:T(8,128)(2,1)S(1)}, u32[]{:S(2)}, u32[]{:S(2)}) %collective-permute-start.16) | collective-permute-done | bytes 262176 | tf_op jit(solution)/shard_map/ppermute | solution.py:26
  18.4 0.3 collective-permute-start.1
  18.8 0.3 collective-permute-done.15.refs_1_
  19.1 0.7 copy-done.10
  19.8 1.6 %collective-permute-start.25 = (bf16[4,128,256]{2,1,0:T(8,128)(2,1)S(1)}, bf16[4,128,256]{2,1,0:T(8,128)(2,1)}, u32[]{:S(2)}, u32[]{:S(2)}) collective-permute-start(bf16[4,128,256]{2,1,0:T(8,128)(2,1)S(1)} %collective-permute-done.23.refs_2_), channel_id=1, source_target_pairs={{0,2},{1,3},{2,4},{3,5},{4,6},{5,7},{6,0},{7,1},{8,10},{9,11},{10,... | collective-permute-start | bytes 786440 | tf_op jit(solution)/shard_map/ppermute | solution.py:26
  21.4 2.7 %collective-permute-done.9.refs_2_ = bf16[4,128,256]{2,1,0:T(8,128)(2,1)S(1)} collective-permute-done((bf16[4,128,256]{2,1,0:T(8,128)(2,1)S(1)}, bf16[4,128,256]{2,1,0:T(8,128)(2,1)S(1)}, u32[]{:S(2)}, u32[]{:S(2)}) %collective-permute-start.9) | collective-permute-done | bytes 262176 | tf_op jit(solution)/shard_map/ppermute | solution.py:26
  24.1 1.9 %collective-permute-start.24 = (bf16[4,128,256]{2,1,0:T(8,128)(2,1)S(1)}, bf16[4,128,256]{2,1,0:T(8,128)(2,1)S(1)}, u32[]{:S(2)}, u32[]{:S(2)}) collective-permute-start(bf16[4,128,256]{2,1,0:T(8,128)(2,1)S(1)} %collective-permute-done.23.refs_2_), channel_id=1, source_target_pairs={{0,1},{1,0},{2,3},{3,2},{4,5},{5,4},{6,7},{7,6},{8,9},{9,8},{10,11... | collective-permute-start | bytes 786440 | tf_op jit(solution)/shard_map/ppermute | solution.py:26
  26.0 0.0 collective-permute-done.8.refs_1_
  26.0 0.7 copy-done.14
  26.7 0.3 collective-permute-start.18
  27.0 2.7 %collective-permute-done.1.refs_2_ = bf16[4,128,256]{2,1,0:T(8,128)(2,1)S(1)} collective-permute-done((bf16[4,128,256]{2,1,0:T(8,128)(2,1)S(1)}, bf16[4,128,256]{2,1,0:T(8,128)(2,1)S(1)}, u32[]{:S(2)}, u32[]{:S(2)}) %collective-permute-start.1) | collective-permute-done | bytes 262176 | tf_op jit(solution)/shard_map/ppermute | solution.py:26
  29.7 1.9 %collective-permute-start.17 = (bf16[4,128,256]{2,1,0:T(8,128)(2,1)S(1)}, bf16[4,128,256]{2,1,0:T(8,128)(2,1)S(1)}, u32[]{:S(2)}, u32[]{:S(2)}) collective-permute-start(bf16[4,128,256]{2,1,0:T(8,128)(2,1)S(1)} %collective-permute-done.16.refs_2_), channel_id=1, source_target_pairs={{0,1},{1,0},{2,3},{3,2},{4,5},{5,4},{6,7},{7,6},{8,9},{9,8},{10,11... | collective-permute-start | bytes 786440 | tf_op jit(solution)/shard_map/ppermute | solution.py:26
  31.6 0.7 copy-done.8
  32.3 3.1 %collective-permute-done.25.refs_4_ = bf16[4,128,256]{2,1,0:T(8,128)(2,1)} collective-permute-done((bf16[4,128,256]{2,1,0:T(8,128)(2,1)S(1)}, bf16[4,128,256]{2,1,0:T(8,128)(2,1)}, u32[]{:S(2)}, u32[]{:S(2)}) %collective-permute-start.25) | collective-permute-done | bytes 262176 | tf_op jit(solution)/shard_map/ppermute | solution.py:26
  35.4 0.3 collective-permute-start.11
  35.7 0.0 collective-permute-done.24.refs_3_
  35.7 0.7 copy-done.4
  36.4 1.6 %collective-permute-start.10 = (bf16[4,128,256]{2,1,0:T(8,128)(2,1)S(1)}, bf16[4,128,256]{2,1,0:T(8,128)(2,1)S(1)}, u32[]{:S(2)}, u32[]{:S(2)}) collective-permute-start(bf16[4,128,256]{2,1,0:T(8,128)(2,1)S(1)} %collective-permute-done.9.refs_2_), channel_id=1, source_target_pairs={{0,1},{1,0},{2,3},{3,2},{4,5},{5,4},{6,7},{7,6},{8,9},{9,8},{10,11... | collective-permute-start | bytes 786440 | tf_op jit(solution)/shard_map/ppermute | solution.py:26
  38.1 0.7 copy-done.12
  38.8 2.3 %collective-permute-done.18.refs_4_ = bf16[4,128,256]{2,1,0:T(8,128)(2,1)} collective-permute-done((bf16[4,128,256]{2,1,0:T(8,128)(2,1)S(1)}, bf16[4,128,256]{2,1,0:T(8,128)(2,1)}, u32[]{:S(2)}, u32[]{:S(2)}) %collective-permute-start.18) | collective-permute-done | bytes 262176 | tf_op jit(solution)/shard_map/ppermute | solution.py:26
  41.0 0.3 collective-permute-start.3
  41.3 0.7 copy-done.18
  42.0 1.6 %collective-permute-start.27 = (bf16[4,128,256]{2,1,0:T(8,128)(2,1)}, bf16[4,128,256]{2,1,0:T(8,128)(2,1)}, u32[]{:S(2)}, u32[]{:S(2)}) collective-permute-start(bf16[4,128,256]{2,1,0:T(8,128)(2,1)} %collective-permute-done.25.refs_4_), channel_id=1, source_target_pairs={{0,2},{1,3},{2,4},{3,5},{4,6},{5,7},{6,0},{7,1},{8,10},{9,11},{10,... | collective-permute-start | bytes 786440 | tf_op jit(solution)/shard_map/ppermute | solution.py:26
  43.6 3.0 %collective-permute-done.11.refs_4_ = bf16[4,128,256]{2,1,0:T(8,128)(2,1)} collective-permute-done((bf16[4,128,256]{2,1,0:T(8,128)(2,1)S(1)}, bf16[4,128,256]{2,1,0:T(8,128)(2,1)}, u32[]{:S(2)}, u32[]{:S(2)}) %collective-permute-start.11) | collective-permute-done | bytes 262176 | tf_op jit(solution)/shard_map/ppermute | solution.py:26
  46.6 1.9 %collective-permute-start.26 = (bf16[4,128,256]{2,1,0:T(8,128)(2,1)}, bf16[4,128,256]{2,1,0:T(8,128)(2,1)}, u32[]{:S(2)}, u32[]{:S(2)}) collective-permute-start(bf16[4,128,256]{2,1,0:T(8,128)(2,1)} %collective-permute-done.25.refs_4_), channel_id=1, source_target_pairs={{0,1},{1,0},{2,3},{3,2},{4,5},{5,4},{6,7},{7,6},{8,9},{9,8},{10,11... | collective-permute-start | bytes 786440 | tf_op jit(solution)/shard_map/ppermute | solution.py:26
  48.6 0.7 copy-done.20
  49.3 2.8 %collective-permute-done.3.refs_4_ = bf16[4,128,256]{2,1,0:T(8,128)(2,1)S(1)} collective-permute-done((bf16[4,128,256]{2,1,0:T(8,128)(2,1)S(1)}, bf16[4,128,256]{2,1,0:T(8,128)(2,1)S(1)}, u32[]{:S(2)}, u32[]{:S(2)}) %collective-permute-start.3) | collective-permute-done | bytes 262176 | tf_op jit(solution)/shard_map/ppermute | solution.py:26
  52.2 0.7 copy-done.16
  52.9 0.3 collective-permute-start.13
  53.2 4.7 %collective-permute-done.27.refs_6_ = bf16[4,128,256]{2,1,0:T(8,128)(2,1)} collective-permute-done((bf16[4,128,256]{2,1,0:T(8,128)(2,1)}, bf16[4,128,256]{2,1,0:T(8,128)(2,1)}, u32[]{:S(2)}, u32[]{:S(2)}) %collective-permute-start.27) | collective-permute-done | bytes 262176 | tf_op jit(solution)/shard_map/ppermute | solution.py:26
  57.9 1.9 %collective-permute-start.28 = (bf16[4,128,256]{2,1,0:T(8,128)(2,1)}, bf16[4,128,256]{2,1,0:T(8,128)(2,1)}, u32[]{:S(2)}, u32[]{:S(2)}) collective-permute-start(bf16[4,128,256]{2,1,0:T(8,128)(2,1)} %collective-permute-done.27.refs_6_), channel_id=1, source_target_pairs={{0,1},{1,0},{2,3},{3,2},{4,5},{5,4},{6,7},{7,6},{8,9},{9,8},{10,11... | collective-permute-start | bytes 786440 | tf_op jit(solution)/shard_map/ppermute | solution.py:26
  59.9 0.1 collective-permute-start.19
  60.0 3.5 %collective-permute-done.20.refs_6_ = bf16[4,128,256]{2,1,0:T(8,128)(2,1)} collective-permute-done((bf16[4,128,256]{2,1,0:T(8,128)(2,1)}, bf16[4,128,256]{2,1,0:T(8,128)(2,1)}, u32[]{:S(2)}, u32[]{:S(2)}) %collective-permute-start.20) | collective-permute-done | bytes 262176 | tf_op jit(solution)/shard_map/ppermute | solution.py:26
  63.5 1.9 %collective-permute-start.12 = (bf16[4,128,256]{2,1,0:T(8,128)(2,1)}, bf16[4,128,256]{2,1,0:T(8,128)(2,1)S(1)}, u32[]{:S(2)}, u32[]{:S(2)}) collective-permute-start(bf16[4,128,256]{2,1,0:T(8,128)(2,1)} %collective-permute-done.11.refs_4_), channel_id=1, source_target_pairs={{0,1},{1,0},{2,3},{3,2},{4,5},{5,4},{6,7},{7,6},{8,9},{9,8},{10,11... | collective-permute-start | bytes 786440 | tf_op jit(solution)/shard_map/ppermute | solution.py:26
  65.4 3.7 %collective-permute-done.13.refs_6_ = bf16[4,128,256]{2,1,0:T(8,128)(2,1)} collective-permute-done((bf16[4,128,256]{2,1,0:T(8,128)(2,1)}, bf16[4,128,256]{2,1,0:T(8,128)(2,1)}, u32[]{:S(2)}, u32[]{:S(2)}) %collective-permute-start.13) | collective-permute-done | bytes 262176 | tf_op jit(solution)/shard_map/ppermute | solution.py:26
  69.1 0.3 collective-permute-start.5
  69.4 0.0 collective-permute-done.28.refs_7_
  69.4 1.6 %collective-permute-start.21 = (bf16[4,128,256]{2,1,0:T(8,128)(2,1)}, bf16[4,128,256]{2,1,0:T(8,128)(2,1)S(1)}, u32[]{:S(2)}, u32[]{:S(2)}) collective-permute-start(bf16[4,128,256]{2,1,0:T(8,128)(2,1)} %collective-permute-done.20.refs_6_), channel_id=1, source_target_pairs={{0,1},{1,0},{2,3},{3,2},{4,5},{5,4},{6,7},{7,6},{8,9},{9,8},{10,11... | collective-permute-start | bytes 786440 | tf_op jit(solution)/shard_map/ppermute | solution.py:26
  71.1 0.1 compare_reduce_fusion
  71.2 0.5 collective-permute-start.14
  71.6 2.2 %copy-done.1 = bf16[1,2,128,8192]{3,2,1,0:T(8,128)(2,1)S(1)} copy-done((bf16[1,2,128,8192]{3,2,1,0:T(8,128)(2,1)S(1)}, bf16[1,2,128,8192]{3,2,1,0:T(8,128)(2,1)}, u32[]{:S(2)}) %copy-start.1) | copy-done | bytes 4194328
  73.8 0.9 copy-done.3
  74.8 0.9 copy-done.5
  75.8 8.4 %shard_map.55.refs_9_ = f32[128,8192]{1,0:T(8,128)} custom-call(s32[2,8,8]{2,1,0:T(8,128)S(1)} %convert_element_type.3.live_ref, bf16[2,128,8192]{2,1,0:T(8,128)(2,1)S(1)} %bitcast.22, bf16[4,128,256]{2,1,0:T(8,128)(2,1)S(1)} %pad_maximum_fusion.3.refs_0_, bf16[4,128,256]{2,1,0:T(8,128)(2,1)S(1)} %copy-done.3, ...), custom_call_target="tpu_custom_call" | custom-call | flops 2147483648 | bytes 2621440 | tf_op jit(solution)/shard_map/pallas_call | solution.py:100
  84.2 1.7 %collective-permute-start = (bf16[4,128,256]{2,1,0:T(8,128)(2,1)S(1)}, bf16[4,128,256]{2,1,0:T(8,128)(2,1)S(1)}, u32[]{:S(2)}, u32[]{:S(2)}) collective-permute-start(bf16[4,128,256]{2,1,0:T(8,128)(2,1)S(1)} %pad_maximum_fusion.refs_0_), channel_id=1, source_target_pairs={{0,1},{1,0},{2,3},{3,2},{4,5},{5,4},{6,7},{7,6},{8,9},{9,8},{10,11... | collective-permute-start | bytes 786440 | tf_op jit(solution)/shard_map/ppermute | solution.py:26
  85.9 0.4 collective-permute-start.2
  86.3 1.6 %collective-permute-start.4 = (bf16[4,128,256]{2,1,0:T(8,128)(2,1)S(1)}, bf16[4,128,256]{2,1,0:T(8,128)(2,1)S(1)}, u32[]{:S(2)}, u32[]{:S(2)}) collective-permute-start(bf16[4,128,256]{2,1,0:T(8,128)(2,1)S(1)} %copy-done.17), channel_id=1, source_target_pairs={{0,1},{1,0},{2,3},{3,2},{4,5},{5,4},{6,7},{7,6},{8,9},{9,8},{10,11... | collective-permute-start | bytes 786440 | tf_op jit(solution)/shard_map/ppermute | solution.py:26
  87.9 0.4 collective-permute-start.6
  88.3 8.3 %shard_map.56.refs_9_ = f32[128,8192]{1,0:T(8,128)} custom-call(s32[2,8,8]{2,1,0:T(8,128)S(1)} %convert_element_type.3.live_ref, bf16[2,128,8192]{2,1,0:T(8,128)(2,1)S(1)} %bitcast.23, bf16[4,128,256]{2,1,0:T(8,128)(2,1)S(1)} %pad_maximum_fusion.2.refs_0_, bf16[4,128,256]{2,1,0:T(8,128)(2,1)S(1)} %copy-done.11, ...), custom_call_target="tpu_custom_call", output_to_operand_aliasing={{}: (11, {})} | custom-call | flops 2147483648 | bytes 2621440 | tf_op jit(solution)/shard_map/pallas_call | solution.py:100
  96.6 8.3 %shard_map.57.refs_9_ = f32[128,8192]{1,0:T(8,128)} custom-call(s32[2,8,8]{2,1,0:T(8,128)S(1)} %convert_element_type.3.live_ref, bf16[2,128,8192]{2,1,0:T(8,128)(2,1)S(1)} %bitcast.24, bf16[4,128,256]{2,1,0:T(8,128)(2,1)S(1)} %pad_maximum_fusion.1.refs_0_, bf16[4,128,256]{2,1,0:T(8,128)(2,1)S(1)} %copy-done.15, ...), custom_call_target="tpu_custom_call", output_to_operand_aliasing={{}: (11, {})} | custom-call | flops 2147483648 | bytes 2621440 | tf_op jit(solution)/shard_map/pallas_call | solution.py:100
  104.9 0.8 collective-permute-done.4.refs_5_
  105.7 5.6 %collective-permute-done.6.refs_7_ = bf16[4,128,256]{2,1,0:T(8,128)(2,1)S(1)} collective-permute-done((bf16[4,128,256]{2,1,0:T(8,128)(2,1)S(1)}, bf16[4,128,256]{2,1,0:T(8,128)(2,1)S(1)}, u32[]{:S(2)}, u32[]{:S(2)}) %collective-permute-start.6) | collective-permute-done | bytes 262176 | tf_op jit(solution)/shard_map/ppermute | solution.py:26
  111.3 7.9 %shard_map.58 = f32[128,8192]{1,0:T(8,128)} custom-call(s32[2,8,8]{2,1,0:T(8,128)S(1)} %convert_element_type.3.live_ref, bf16[2,128,8192]{2,1,0:T(8,128)(2,1)S(1)} %bitcast.25, bf16[4,128,256]{2,1,0:T(8,128)(2,1)S(1)} %pad_maximum_fusion.refs_0_, bf16[4,128,256]{2,1,0:T(8,128)(2,1)S(1)} %collective-permute-done.refs_1_, ...), custom_call_target="tpu_custom_call", output_to_operand_aliasing={{}: (11, {})} | custom-call | flops 2147483648 | bytes 2621440 | tf_op jit(solution)/shard_map/pallas_call | solution.py:100
  (51 shorter events, 0.2 us)
Async XLA Ops:
  0.0 59.8 %copy-start = (s32[1,2,8,8,8]{4,3,2,1,0:T(8,128)S(1)}, s32[1,2,8,8,8]{4,3,2,1,0:T(8,128)}, u32[]{:S(2)}) copy-start(s32[1,2,8,8,8]{4,3,2,1,0:T(8,128)} %param.9) | copy-start | bytes 12292
  0.0 71.2 %collective-permute-start.7 = (bf16[128,8192]{1,0:T(8,128)(2,1)}, bf16[128,8192]{1,0:T(8,128)(2,1)S(1)}, u32[]{:S(2)}, u32[]{:S(2)}) collective-permute-start(bf16[128,8192]{1,0:T(8,128)(2,1)} %bitcast.27), channel_id=1, source_target_pairs={{0,8},{8,16},{16,24},{24,0},{1,9},{9,17},{17,25},{25,1},{2,10},{10... | collective-permute-start | bytes 6291464 | tf_op jit(solution)/shard_map/ppermute | solution.py:26
  1.9 10.9 %collective-permute-start.23 = (bf16[4,128,256]{2,1,0:T(8,128)(2,1)S(1)}, bf16[4,128,256]{2,1,0:T(8,128)(2,1)S(1)}, u32[]{:S(2)}, u32[]{:S(2)}) collective-permute-start(bf16[4,128,256]{2,1,0:T(8,128)(2,1)S(1)} %pad_maximum_fusion.3.refs_0_), channel_id=1, source_target_pairs={{0,2},{1,3},{2,4},{3,5},{4,6},{5,7},{6,0},{7,1},{8,10},{9,11},{10,... | collective-permute-start | bytes 786440 | tf_op jit(solution)/shard_map/ppermute | solution.py:26
  4.5 8.9 %collective-permute-start.22 = (bf16[4,128,256]{2,1,0:T(8,128)(2,1)S(1)}, bf16[4,128,256]{2,1,0:T(8,128)(2,1)S(1)}, u32[]{:S(2)}, u32[]{:S(2)}) collective-permute-start(bf16[4,128,256]{2,1,0:T(8,128)(2,1)S(1)} %pad_maximum_fusion.3.refs_0_), channel_id=1, source_target_pairs={{0,1},{1,0},{2,3},{3,2},{4,5},{5,4},{6,7},{7,6},{8,9},{9,8},{10,11... | collective-permute-start | bytes 786440 | tf_op jit(solution)/shard_map/ppermute | solution.py:26
  6.1 12.4 %collective-permute-start.16 = (bf16[4,128,256]{2,1,0:T(8,128)(2,1)S(1)}, bf16[4,128,256]{2,1,0:T(8,128)(2,1)S(1)}, u32[]{:S(2)}, u32[]{:S(2)}) collective-permute-start(bf16[4,128,256]{2,1,0:T(8,128)(2,1)S(1)} %pad_maximum_fusion.2.refs_0_), channel_id=1, source_target_pairs={{0,2},{1,3},{2,4},{3,5},{4,6},{5,7},{6,0},{7,1},{8,10},{9,11},{10,... | collective-permute-start | bytes 786440 | tf_op jit(solution)/shard_map/ppermute | solution.py:26
  7.7 11.4 %collective-permute-start.15 = (bf16[4,128,256]{2,1,0:T(8,128)(2,1)S(1)}, bf16[4,128,256]{2,1,0:T(8,128)(2,1)S(1)}, u32[]{:S(2)}, u32[]{:S(2)}) collective-permute-start(bf16[4,128,256]{2,1,0:T(8,128)(2,1)S(1)} %pad_maximum_fusion.2.refs_0_), channel_id=1, source_target_pairs={{0,1},{1,0},{2,3},{3,2},{4,5},{5,4},{6,7},{7,6},{8,9},{9,8},{10,11... | collective-permute-start | bytes 786440 | tf_op jit(solution)/shard_map/ppermute | solution.py:26
  12.8 11.2 %collective-permute-start.9 = (bf16[4,128,256]{2,1,0:T(8,128)(2,1)S(1)}, bf16[4,128,256]{2,1,0:T(8,128)(2,1)S(1)}, u32[]{:S(2)}, u32[]{:S(2)}) collective-permute-start(bf16[4,128,256]{2,1,0:T(8,128)(2,1)S(1)} %pad_maximum_fusion.1.refs_0_), channel_id=1, source_target_pairs={{0,2},{1,3},{2,4},{3,5},{4,6},{5,7},{6,0},{7,1},{8,10},{9,11},{10,... | collective-permute-start | bytes 786440 | tf_op jit(solution)/shard_map/ppermute | solution.py:26
  13.5 0.7 copy-start.2
  14.2 11.9 %collective-permute-start.8 = (bf16[4,128,256]{2,1,0:T(8,128)(2,1)S(1)}, bf16[4,128,256]{2,1,0:T(8,128)(2,1)S(1)}, u32[]{:S(2)}, u32[]{:S(2)}) collective-permute-start(bf16[4,128,256]{2,1,0:T(8,128)(2,1)S(1)} %pad_maximum_fusion.1.refs_0_), channel_id=1, source_target_pairs={{0,1},{1,0},{2,3},{3,2},{4,5},{5,4},{6,7},{7,6},{8,9},{9,8},{10,11... | collective-permute-start | bytes 786440 | tf_op jit(solution)/shard_map/ppermute | solution.py:26
  18.4 11.2 %collective-permute-start.1 = (bf16[4,128,256]{2,1,0:T(8,128)(2,1)S(1)}, bf16[4,128,256]{2,1,0:T(8,128)(2,1)S(1)}, u32[]{:S(2)}, u32[]{:S(2)}) collective-permute-start(bf16[4,128,256]{2,1,0:T(8,128)(2,1)S(1)} %pad_maximum_fusion.refs_0_), channel_id=1, source_target_pairs={{0,2},{1,3},{2,4},{3,5},{4,6},{5,7},{6,0},{7,1},{8,10},{9,11},{10,... | collective-permute-start | bytes 786440 | tf_op jit(solution)/shard_map/ppermute | solution.py:26
  19.1 0.7 copy-start.10
  19.8 15.6 %collective-permute-start.25 = (bf16[4,128,256]{2,1,0:T(8,128)(2,1)S(1)}, bf16[4,128,256]{2,1,0:T(8,128)(2,1)}, u32[]{:S(2)}, u32[]{:S(2)}) collective-permute-start(bf16[4,128,256]{2,1,0:T(8,128)(2,1)S(1)} %collective-permute-done.23.refs_2_), channel_id=1, source_target_pairs={{0,2},{1,3},{2,4},{3,5},{4,6},{5,7},{6,0},{7,1},{8,10},{9,11},{10,... | collective-permute-start | bytes 786440 | tf_op jit(solution)/shard_map/ppermute | solution.py:26
  24.1 11.7 %collective-permute-start.24 = (bf16[4,128,256]{2,1,0:T(8,128)(2,1)S(1)}, bf16[4,128,256]{2,1,0:T(8,128)(2,1)S(1)}, u32[]{:S(2)}, u32[]{:S(2)}) collective-permute-start(bf16[4,128,256]{2,1,0:T(8,128)(2,1)S(1)} %collective-permute-done.23.refs_2_), channel_id=1, source_target_pairs={{0,1},{1,0},{2,3},{3,2},{4,5},{5,4},{6,7},{7,6},{8,9},{9,8},{10,11... | collective-permute-start | bytes 786440 | tf_op jit(solution)/shard_map/ppermute | solution.py:26
  26.0 0.7 copy-start.14
  26.7 14.3 %collective-permute-start.18 = (bf16[4,128,256]{2,1,0:T(8,128)(2,1)S(1)}, bf16[4,128,256]{2,1,0:T(8,128)(2,1)}, u32[]{:S(2)}, u32[]{:S(2)}) collective-permute-start(bf16[4,128,256]{2,1,0:T(8,128)(2,1)S(1)} %collective-permute-done.16.refs_2_), channel_id=1, source_target_pairs={{0,2},{1,3},{2,4},{3,5},{4,6},{5,7},{6,0},{7,1},{8,10},{9,11},{10,... | collective-permute-start | bytes 786440 | tf_op jit(solution)/shard_map/ppermute | solution.py:26
  29.7 11.3 %copy-start.6 = (bf16[4,128,256]{2,1,0:T(8,128)(2,1)}, bf16[4,128,256]{2,1,0:T(8,128)(2,1)S(1)}, u32[]{:S(2)}) copy-start(bf16[4,128,256]{2,1,0:T(8,128)(2,1)S(1)} %collective-permute-done.1.refs_2_) | copy-start | bytes 786436
  29.7 11.7 %collective-permute-start.17 = (bf16[4,128,256]{2,1,0:T(8,128)(2,1)S(1)}, bf16[4,128,256]{2,1,0:T(8,128)(2,1)S(1)}, u32[]{:S(2)}, u32[]{:S(2)}) collective-permute-start(bf16[4,128,256]{2,1,0:T(8,128)(2,1)S(1)} %collective-permute-done.16.refs_2_), channel_id=1, source_target_pairs={{0,1},{1,0},{2,3},{3,2},{4,5},{5,4},{6,7},{7,6},{8,9},{9,8},{10,11... | collective-permute-start | bytes 786440 | tf_op jit(solution)/shard_map/ppermute | solution.py:26
  31.6 0.7 copy-start.8
  35.4 11.2 %collective-permute-start.11 = (bf16[4,128,256]{2,1,0:T(8,128)(2,1)S(1)}, bf16[4,128,256]{2,1,0:T(8,128)(2,1)}, u32[]{:S(2)}, u32[]{:S(2)}) collective-permute-start(bf16[4,128,256]{2,1,0:T(8,128)(2,1)S(1)} %collective-permute-done.9.refs_2_), channel_id=1, source_target_pairs={{0,2},{1,3},{2,4},{3,5},{4,6},{5,7},{6,0},{7,1},{8,10},{9,11},{10,... | collective-permute-start | bytes 786440 | tf_op jit(solution)/shard_map/ppermute | solution.py:26
  35.7 0.7 copy-start.4
  36.4 12.2 %collective-permute-start.10 = (bf16[4,128,256]{2,1,0:T(8,128)(2,1)S(1)}, bf16[4,128,256]{2,1,0:T(8,128)(2,1)S(1)}, u32[]{:S(2)}, u32[]{:S(2)}) collective-permute-start(bf16[4,128,256]{2,1,0:T(8,128)(2,1)S(1)} %collective-permute-done.9.refs_2_), channel_id=1, source_target_pairs={{0,1},{1,0},{2,3},{3,2},{4,5},{5,4},{6,7},{7,6},{8,9},{9,8},{10,11... | collective-permute-start | bytes 786440 | tf_op jit(solution)/shard_map/ppermute | solution.py:26
  38.1 0.7 copy-start.12
  41.0 11.1 %collective-permute-start.3 = (bf16[4,128,256]{2,1,0:T(8,128)(2,1)S(1)}, bf16[4,128,256]{2,1,0:T(8,128)(2,1)S(1)}, u32[]{:S(2)}, u32[]{:S(2)}) collective-permute-start(bf16[4,128,256]{2,1,0:T(8,128)(2,1)S(1)} %collective-permute-done.1.refs_2_), channel_id=1, source_target_pairs={{0,2},{1,3},{2,4},{3,5},{4,6},{5,7},{6,0},{7,1},{8,10},{9,11},{10,... | collective-permute-start | bytes 786440 | tf_op jit(solution)/shard_map/ppermute | solution.py:26
  41.3 0.7 copy-start.18
  42.0 15.8 %collective-permute-start.27 = (bf16[4,128,256]{2,1,0:T(8,128)(2,1)}, bf16[4,128,256]{2,1,0:T(8,128)(2,1)}, u32[]{:S(2)}, u32[]{:S(2)}) collective-permute-start(bf16[4,128,256]{2,1,0:T(8,128)(2,1)} %collective-permute-done.25.refs_4_), channel_id=1, source_target_pairs={{0,2},{1,3},{2,4},{3,5},{4,6},{5,7},{6,0},{7,1},{8,10},{9,11},{10,... | collective-permute-start | bytes 786440 | tf_op jit(solution)/shard_map/ppermute | solution.py:26
  46.6 13.2 %collective-permute-start.26 = (bf16[4,128,256]{2,1,0:T(8,128)(2,1)}, bf16[4,128,256]{2,1,0:T(8,128)(2,1)}, u32[]{:S(2)}, u32[]{:S(2)}) collective-permute-start(bf16[4,128,256]{2,1,0:T(8,128)(2,1)} %collective-permute-done.25.refs_4_), channel_id=1, source_target_pairs={{0,1},{1,0},{2,3},{3,2},{4,5},{5,4},{6,7},{7,6},{8,9},{9,8},{10,11... | collective-permute-start | bytes 786440 | tf_op jit(solution)/shard_map/ppermute | solution.py:26
  48.6 0.7 copy-start.20
  49.3 14.2 %collective-permute-start.20 = (bf16[4,128,256]{2,1,0:T(8,128)(2,1)}, bf16[4,128,256]{2,1,0:T(8,128)(2,1)}, u32[]{:S(2)}, u32[]{:S(2)}) collective-permute-start(bf16[4,128,256]{2,1,0:T(8,128)(2,1)} %collective-permute-done.18.refs_4_), channel_id=1, source_target_pairs={{0,2},{1,3},{2,4},{3,5},{4,6},{5,7},{6,0},{7,1},{8,10},{9,11},{10,... | collective-permute-start | bytes 786440 | tf_op jit(solution)/shard_map/ppermute | solution.py:26
  52.2 0.7 copy-start.16
  52.9 16.3 %collective-permute-start.13 = (bf16[4,128,256]{2,1,0:T(8,128)(2,1)}, bf16[4,128,256]{2,1,0:T(8,128)(2,1)}, u32[]{:S(2)}, u32[]{:S(2)}) collective-permute-start(bf16[4,128,256]{2,1,0:T(8,128)(2,1)} %collective-permute-done.11.refs_4_), channel_id=1, source_target_pairs={{0,2},{1,3},{2,4},{3,5},{4,6},{5,7},{6,0},{7,1},{8,10},{9,11},{10,... | collective-permute-start | bytes 786440 | tf_op jit(solution)/shard_map/ppermute | solution.py:26
  57.9 11.6 %collective-permute-start.28 = (bf16[4,128,256]{2,1,0:T(8,128)(2,1)}, bf16[4,128,256]{2,1,0:T(8,128)(2,1)}, u32[]{:S(2)}, u32[]{:S(2)}) collective-permute-start(bf16[4,128,256]{2,1,0:T(8,128)(2,1)} %collective-permute-done.27.refs_6_), channel_id=1, source_target_pairs={{0,1},{1,0},{2,3},{3,2},{4,5},{5,4},{6,7},{7,6},{8,9},{9,8},{10,11... | collective-permute-start | bytes 786440 | tf_op jit(solution)/shard_map/ppermute | solution.py:26
  59.9 24.3 %collective-permute-start.19 = (bf16[4,128,256]{2,1,0:T(8,128)(2,1)}, bf16[4,128,256]{2,1,0:T(8,128)(2,1)S(1)}, u32[]{:S(2)}, u32[]{:S(2)}) collective-permute-start(bf16[4,128,256]{2,1,0:T(8,128)(2,1)} %collective-permute-done.18.refs_4_), channel_id=1, source_target_pairs={{0,1},{1,0},{2,3},{3,2},{4,5},{5,4},{6,7},{7,6},{8,9},{9,8},{10,11... | collective-permute-start | bytes 786440 | tf_op jit(solution)/shard_map/ppermute | solution.py:26
  63.5 22.4 %collective-permute-start.12 = (bf16[4,128,256]{2,1,0:T(8,128)(2,1)}, bf16[4,128,256]{2,1,0:T(8,128)(2,1)S(1)}, u32[]{:S(2)}, u32[]{:S(2)}) collective-permute-start(bf16[4,128,256]{2,1,0:T(8,128)(2,1)} %collective-permute-done.11.refs_4_), channel_id=1, source_target_pairs={{0,1},{1,0},{2,3},{3,2},{4,5},{5,4},{6,7},{7,6},{8,9},{9,8},{10,11... | collective-permute-start | bytes 786440 | tf_op jit(solution)/shard_map/ppermute | solution.py:26
  69.1 17.2 %collective-permute-start.5 = (bf16[4,128,256]{2,1,0:T(8,128)(2,1)}, bf16[4,128,256]{2,1,0:T(8,128)(2,1)S(1)}, u32[]{:S(2)}, u32[]{:S(2)}) collective-permute-start(bf16[4,128,256]{2,1,0:T(8,128)(2,1)} %copy-done.16), channel_id=1, source_target_pairs={{0,2},{1,3},{2,4},{3,5},{4,6},{5,7},{6,0},{7,1},{8,10},{9,11},{10,... | collective-permute-start | bytes 786440 | tf_op jit(solution)/shard_map/ppermute | solution.py:26
  69.4 18.5 %collective-permute-start.21 = (bf16[4,128,256]{2,1,0:T(8,128)(2,1)}, bf16[4,128,256]{2,1,0:T(8,128)(2,1)S(1)}, u32[]{:S(2)}, u32[]{:S(2)}) collective-permute-start(bf16[4,128,256]{2,1,0:T(8,128)(2,1)} %collective-permute-done.20.refs_6_), channel_id=1, source_target_pairs={{0,1},{1,0},{2,3},{3,2},{4,5},{5,4},{6,7},{7,6},{8,9},{9,8},{10,11... | collective-permute-start | bytes 786440 | tf_op jit(solution)/shard_map/ppermute | solution.py:26
  71.2 25.4 %collective-permute-start.14 = (bf16[4,128,256]{2,1,0:T(8,128)(2,1)}, bf16[4,128,256]{2,1,0:T(8,128)(2,1)S(1)}, u32[]{:S(2)}, u32[]{:S(2)}) collective-permute-start(bf16[4,128,256]{2,1,0:T(8,128)(2,1)} %collective-permute-done.13.refs_6_), channel_id=1, source_target_pairs={{0,1},{1,0},{2,3},{3,2},{4,5},{5,4},{6,7},{7,6},{8,9},{9,8},{10,11... | collective-permute-start | bytes 786440 | tf_op jit(solution)/shard_map/ppermute | solution.py:26
  71.6 2.2 %copy-start.1 = (bf16[1,2,128,8192]{3,2,1,0:T(8,128)(2,1)S(1)}, bf16[1,2,128,8192]{3,2,1,0:T(8,128)(2,1)}, u32[]{:S(2)}) copy-start(bf16[1,2,128,8192]{3,2,1,0:T(8,128)(2,1)} %param.6) | copy-start | bytes 12582916
  73.8 0.9 copy-start.3
  74.8 0.9 copy-start.5
  75.7 10.1 %copy-start.7 = (bf16[4,128,256]{2,1,0:T(8,128)(2,1)S(1)}, bf16[4,128,256]{2,1,0:T(8,128)(2,1)}, u32[]{:S(2)}) copy-start(bf16[4,128,256]{2,1,0:T(8,128)(2,1)} %copy-done.6) | copy-start | bytes 786436
  75.7 10.5 %copy-start.17 = (bf16[4,128,256]{2,1,0:T(8,128)(2,1)S(1)}, bf16[4,128,256]{2,1,0:T(8,128)(2,1)}, u32[]{:S(2)}) copy-start(bf16[4,128,256]{2,1,0:T(8,128)(2,1)} %copy-done.16) | copy-start | bytes 786436
  75.7 12.6 %copy-start.9 = (bf16[4,128,256]{2,1,0:T(8,128)(2,1)S(1)}, bf16[4,128,256]{2,1,0:T(8,128)(2,1)}, u32[]{:S(2)}) copy-start(bf16[4,128,256]{2,1,0:T(8,128)(2,1)} %copy-done.8) | copy-start | bytes 786436
  75.7 12.6 %copy-start.11 = (bf16[4,128,256]{2,1,0:T(8,128)(2,1)S(1)}, bf16[4,128,256]{2,1,0:T(8,128)(2,1)}, u32[]{:S(2)}) copy-start(bf16[4,128,256]{2,1,0:T(8,128)(2,1)} %copy-done.10) | copy-start | bytes 786436
  75.7 12.6 %copy-start.19 = (bf16[4,128,256]{2,1,0:T(8,128)(2,1)S(1)}, bf16[4,128,256]{2,1,0:T(8,128)(2,1)}, u32[]{:S(2)}) copy-start(bf16[4,128,256]{2,1,0:T(8,128)(2,1)} %copy-done.18) | copy-start | bytes 786436
  84.1 12.4 %copy-start.13 = (bf16[4,128,256]{2,1,0:T(8,128)(2,1)S(1)}, bf16[4,128,256]{2,1,0:T(8,128)(2,1)}, u32[]{:S(2)}) copy-start(bf16[4,128,256]{2,1,0:T(8,128)(2,1)} %copy-done.12) | copy-start | bytes 786436
  84.1 12.4 %copy-start.15 = (bf16[4,128,256]{2,1,0:T(8,128)(2,1)S(1)}, bf16[4,128,256]{2,1,0:T(8,128)(2,1)}, u32[]{:S(2)}) copy-start(bf16[4,128,256]{2,1,0:T(8,128)(2,1)} %copy-done.14) | copy-start | bytes 786436
  84.2 12.4 %copy-start.21 = (bf16[4,128,256]{2,1,0:T(8,128)(2,1)S(1)}, bf16[4,128,256]{2,1,0:T(8,128)(2,1)}, u32[]{:S(2)}) copy-start(bf16[4,128,256]{2,1,0:T(8,128)(2,1)} %copy-done.20) | copy-start | bytes 786436
  84.2 20.7 %collective-permute-start = (bf16[4,128,256]{2,1,0:T(8,128)(2,1)S(1)}, bf16[4,128,256]{2,1,0:T(8,128)(2,1)S(1)}, u32[]{:S(2)}, u32[]{:S(2)}) collective-permute-start(bf16[4,128,256]{2,1,0:T(8,128)(2,1)S(1)} %pad_maximum_fusion.refs_0_), channel_id=1, source_target_pairs={{0,1},{1,0},{2,3},{3,2},{4,5},{5,4},{6,7},{7,6},{8,9},{9,8},{10,11... | collective-permute-start | bytes 786440 | tf_op jit(solution)/shard_map/ppermute | solution.py:26
  85.9 19.0 %collective-permute-start.2 = (bf16[4,128,256]{2,1,0:T(8,128)(2,1)S(1)}, bf16[4,128,256]{2,1,0:T(8,128)(2,1)S(1)}, u32[]{:S(2)}, u32[]{:S(2)}) collective-permute-start(bf16[4,128,256]{2,1,0:T(8,128)(2,1)S(1)} %copy-done.7), channel_id=1, source_target_pairs={{0,1},{1,0},{2,3},{3,2},{4,5},{5,4},{6,7},{7,6},{8,9},{9,8},{10,11... | collective-permute-start | bytes 786440 | tf_op jit(solution)/shard_map/ppermute | solution.py:26
  86.3 19.4 %collective-permute-start.4 = (bf16[4,128,256]{2,1,0:T(8,128)(2,1)S(1)}, bf16[4,128,256]{2,1,0:T(8,128)(2,1)S(1)}, u32[]{:S(2)}, u32[]{:S(2)}) collective-permute-start(bf16[4,128,256]{2,1,0:T(8,128)(2,1)S(1)} %copy-done.17), channel_id=1, source_target_pairs={{0,1},{1,0},{2,3},{3,2},{4,5},{5,4},{6,7},{7,6},{8,9},{9,8},{10,11... | collective-permute-start | bytes 786440 | tf_op jit(solution)/shard_map/ppermute | solution.py:26
  87.9 23.4 %collective-permute-start.6 = (bf16[4,128,256]{2,1,0:T(8,128)(2,1)S(1)}, bf16[4,128,256]{2,1,0:T(8,128)(2,1)S(1)}, u32[]{:S(2)}, u32[]{:S(2)}) collective-permute-start(bf16[4,128,256]{2,1,0:T(8,128)(2,1)S(1)} %collective-permute-done.5.refs_6_), channel_id=1, source_target_pairs={{0,1},{1,0},{2,3},{3,2},{4,5},{5,4},{6,7},{7,6},{8,9},{9,8},{10,11... | collective-permute-start | bytes 786440 | tf_op jit(solution)/shard_map/ppermute | solution.py:26

commit v2 on v1

v2 whole, which is shorter than its diff:
```python
import functools
import math

import jax
import jax.numpy as jnp
from jax import lax
from jax.experimental import pallas as pl
from jax.experimental.pallas import tpu as pltpu
from jax.sharding import PartitionSpec as P

HQ = 64
HK = 8
HD = 128
AHEAD = 4
NO_COST = pl.CostEstimate(flops=0, bytes_accessed=0, transcendentals=0)


def columns_of(ring):
    width = 1
    while 2 * (2 * width) ** 2 <= ring:
        width *= 2
    return width


def rotated(array, axis, move):
    size = lax.axis_size(axis)
    return lax.ppermute(array, axis, [(i, move(i)) for i in range(size)])


def tied(array, others):
    if not others:
        return array
    anywhere = pl.BlockSpec(memory_space=pl.ANY)
    return pl.pallas_call(
        lambda *_: None,
        in_specs=[anywhere] * (1 + len(others)),
        out_specs=anywhere,
        out_shape=jax.ShapeDtypeStruct(array.shape, array.dtype),
        input_output_aliases={0: 0},
        cost_estimate=NO_COST,
    )(array, *others)


def attend_body(stage, layers, first_head, places, live_ref, q_ref, *refs):
    operands = 1 + max(operand for _, operand, _ in places)
    kv_refs, refs = refs[:operands], refs[operands:]
    resumes, ends = stage in ("next", "last"), stage in ("whole", "last")
    refs = list(refs)
    carried_ref = refs.pop(0) if ends else None
    before_ref = refs.pop(0) if resumes else None
    if ends:
        _, out_ref = refs
    else:
        (sums_ref,) = refs
    tokens = q_ref.shape[1]
    group = pl.program_id(0)
    factor = math.log2(math.e) / math.sqrt(HD)
    row = lax.broadcasted_iota(jnp.int32, (tokens, tokens), 0)
    col = lax.broadcasted_iota(jnp.int32, (tokens, tokens), 1)
    causal = row >= col
    ones = jnp.ones((tokens, HD), jnp.bfloat16)
    heads = q_ref.shape[2] // HD
    for layer in range(layers):
        visible_key = jnp.broadcast_to(kv_refs[0][layer, 0:1, :], (tokens, HD))
        keys, values, weights = [], [], []
        for place, operand, base in places:
            key = kv_refs[operand][base + layer]
            value = kv_refs[operand][base + layers + layer]
            if place:
                live = live_ref[layer, first_head + group, place] > 0
                keys.append(jnp.where(live, key, visible_key))
                values.append(jnp.where(live, value, jnp.zeros_like(value)))
                weights.append(jnp.where(live, ones, jnp.zeros_like(ones)))
            elif not resumes:
                keys.append(key)
                values.append(value)
                weights.append(ones)
        keys = jnp.concatenate(keys, axis=0)
        values = jnp.concatenate(
            [jnp.concatenate(values, axis=0), jnp.concatenate(weights, axis=0)], axis=1
        )
        for head in range(heads):
            lanes = slice(head * HD, (head + 1) * HD)
            scores = lax.dot_general(
                q_ref[layer, :, lanes],
                keys,
                (((1,), (1,)), ((), ())),
                preferred_element_type=jnp.float32,
            )
            if not resumes:
                own_scores = jnp.where(causal, scores[:, :tokens], -1e30)
                scores = jnp.concatenate([own_scores, scores[:, tokens:]], axis=1)
            row_max = jnp.max(scores, axis=1, keepdims=True)
            if resumes:
                max_before = before_ref[1, layer, :, lanes]
                row_max = jnp.maximum(row_max, max_before)
                shrink = jnp.exp2((max_before - row_max) * factor)
                scores = scores - jnp.concatenate([row_max] * (scores.shape[1] // HD), axis=1)
            else:
                scores = scores - row_max
            weight = jnp.exp2(scores * factor).astype(jnp.bfloat16)
            mixed = jnp.dot(weight, values, preferred_element_type=jnp.float32)
            mixed, total = mixed[:, :HD], mixed[:, HD:]
            if resumes:
                mixed = before_ref[0, layer, :, lanes] * shrink + mixed
                total = shrink + total
            if not ends:
                sums_ref[0, layer, :, lanes] = mixed / total
                sums_ref[1, layer, :, lanes] = row_max + jnp.log2(total) / factor
                continue
            attended = (mixed / total).astype(jnp.bfloat16).astype(jnp.float32)
            if layer:
                attended = out_ref[:, lanes] + attended
            if layer == layers - 1:
                attended = attended.astype(jnp.bfloat16).astype(jnp.float32)
                attended = carried_ref[:, lanes].astype(jnp.float32) + attended
            out_ref[:, lanes] = attended


def attend(stage, live, queries, blocks, carried, before, out, first_head, heads):
    layers, tokens, width = queries.shape
    lanes = width // HK
    anywhere = pl.BlockSpec(memory_space=pl.ANY)
    columns = pl.BlockSpec((tokens, lanes), lambda g, _: (0, first_head + g))
    sums = pl.BlockSpec((2, layers, tokens, lanes), lambda g, _: (0, 0, 0, g))
    arrays, places = [], []
    for place, (array, base) in blocks.items():
        if not any(array is other for other in arrays):
            arrays.append(array)
        places.append((place, [array is other for other in arrays].index(True), base))
    operands = [live, queries, *arrays]
    in_specs = [
        pl.BlockSpec((layers, tokens, lanes), lambda g, _: (0, 0, first_head + g)),
        *[pl.BlockSpec((a.shape[0], tokens, HD), lambda g, _: (0, 0, g)) for a in arrays],
    ]
    aliases = {}
    ends = stage in ("whole", "last")
    if ends:
        operands.append(carried)
        in_specs.append(columns)
    if before is not None:
        operands.append(before)
        in_specs.append(sums)
    if ends:
        if out is not None:
            aliases = {len(operands): 0}
        operands.append(carried if out is None else out)
        in_specs.append(anywhere)
        out_specs = columns
        out_shape = jax.ShapeDtypeStruct((tokens, width), jnp.float32)
    else:
        out_specs = sums
        out_shape = jax.ShapeDtypeStruct((2, layers, tokens, lanes * heads), jnp.float32)
    return pl.pallas_call(
        functools.partial(attend_body, stage, layers, first_head, tuple(places)),
        grid_spec=pltpu.PrefetchScalarGridSpec(
            num_scalar_prefetch=1, grid=(heads,), in_specs=in_specs, out_specs=out_specs
        ),
        out_shape=out_shape,
        input_output_aliases=aliases,
        compiler_params=pltpu.CompilerParams(vmem_limit_bytes=60 << 20),
        cost_estimate=NO_COST,
    )(*operands)


class Stream:
    def __init__(self, block, ring, width):
        self.rows, self.width = ring // width, width
        self.up = lambda i: (i + width) % ring
        self.held, self.across, self.blocks = block, [], {}

    def go(self, step, others=()):
        here = tied(self.held, [*self.across, *others])
        width = self.width
        if step < self.rows - 1:
            self.held = rotated(here, "seq", self.up)
        self.across = [
            rotated(here, "seq", lambda i, by=by: i // width * width + (i + by) % width)
            for by in range(1, width)
        ]
        for by, block in enumerate([here, *self.across]):
            self.blocks[step * width + by] = block, 0


def local(residual, query_rows, key_rows, value_rows, pattern):
    ring = lax.axis_size("seq")
    segments = lax.axis_size("segment")
    width = columns_of(ring)
    rows = ring // width
    me = lax.axis_index("seq")
    carried = rotated(residual[0], "segment", lambda i: (i + 1) % segments)
    place = jnp.arange(ring, dtype=jnp.int32)
    rows_below, shift = place // width, place % width
    held_block = (me // width - rows_below) % rows * width + (me - shift) % width
    chosen = lax.dynamic_index_in_dim(pattern[0], me, axis=2, keepdims=False)
    live = jnp.any(chosen[:, :, :, None] == held_block, axis=2).astype(jnp.int32)

    def stream(first_head, heads):
        lanes = slice(first_head * HD, (first_head + heads) * HD)
        block = jnp.concatenate([key_rows[0, :, :, lanes], value_rows[0, :, :, lanes]], axis=0)
        return Stream(block, ring, width)

    attend_here = functools.partial(attend, live=live, queries=query_rows[0], carried=carried)
    firsts, sizes = (0, AHEAD), (AHEAD, HK - AHEAD)
    streams = [stream(first, size) for first, size in zip(firsts, sizes, strict=True)]
    cut = rows // 2

    def attended(stage, which, steps, state=None, out=None):
        blocks = streams[which].blocks
        blocks = {k: v for k, v in blocks.items() if k // width in steps or (k == 0 and state is not None)}
        return attend_here(
            stage, blocks=blocks, before=state, out=out, first_head=firsts[which], heads=sizes[which]
        )

    states = [None, None]
    for step in range(rows):
        streams[0].go(step, [states[1]] if step == rows - 1 else [])
        if step + 1 == cut:
            states[0] = attended("first", 0, range(cut))
        streams[1].go(step, [states[0]] if step == rows - 2 else [])
        if step + 1 == cut:
            states[1] = attended("first", 1, range(cut))
    out = attended("last", 0, range(cut, rows), states[0])
    out = attended("last", 1, range(cut, rows), states[1], out)
    return out[None]


def solution(mesh):
    return jax.shard_map(
        local,
        mesh=mesh,
        in_specs=(
            P("segment", "seq", None),
            P("segment", None, "seq", None),
            P("segment", None, "seq", None),
            P("segment", None, "seq", None),
            P("segment", None, None, None, None),
        ),
        out_specs=P("segment", "seq", None),
        check_vma=False,
    )
```

time: 120 us -> 109 us (0.908)
  starting transfers between devices: 31.3 us -> 11.3 us
  Pallas kernels: 32.8 us -> 42.3 us
  local copies, waits for them, and re-layouts: 11.9 us -> 5.02 us
  waiting for transfers between devices: 42.8 us -> 49.3 us
    ppermute x29 -> x15, starting transfers between devices: 31.3 us -> 11.3 us  [rotated(): return lax.ppermute(array, axis, [(i, move(i)) for i in range(size)])]
    pallas_call x4 -> x10, Pallas kernels: 32.8 us -> 42.3 us  [the longest x4 42.3 us: attend(): pl.pallas_call(functools.partial(attend_body, stage, layers, first_head,...]
    unnamed x44 -> x16, local copies, waits for them, and re-layouts: 10.5 us -> 3.72 us
    ppermute x29 -> x15, waiting for transfers between devices: 42.8 us -> 49.3 us  [rotated(): return lax.ppermute(array, axis, [(i, move(i)) for i in range(size)])]
  transfers between devices with their start and end apart: 29 -> 15, of which waited for: 15 -> 10; matrix products, arithmetic and copies ran while one was open for 1% -> 1% of each run, Pallas kernels for 21% -> 29%
where the time goes in v2:
time: 109 us
  waiting for transfers between devices  49.3 us (45%)
  Pallas kernels  42.3 us (39%)
  starting transfers between devices  11.3 us (10%)
  local copies, waits for them, and re-layouts  5.02 us (5%)
    ppermute x15, waiting for transfers between devices, rotated(): return lax.ppermute(array, axis, [(i, move(i)) for i in range(size)])  49.3 us
    pallas_call x4, Pallas kernels, attend(): pl.pallas_call(functools.partial(attend_body, stage, layers, first_head,...  42.3 us
    ppermute x15, starting transfers between devices, rotated(): return lax.ppermute(array, axis, [(i, move(i)) for i in range(size)])  11.3 us
    unnamed x16, local copies, waits for them, and re-layouts  3.72 us
  transfers between devices with their start and end apart: 15, of which 10 were waited for; matrix products, arithmetic and copies ran while one was open for 1% of the time, Pallas kernels for 29%

profile of v2, /device:TPU:0, one launch (start us, length us, event | category | flops | bytes accessed | tf_op | source)
XLA Modules:
  0.0 108.9 jit_solution(1091761932487912760)
XLA Ops:
  0.0 0.0 copy-start
  0.0 1.3 %slice_bitcast_fusion = (bf16[2,128,512]{2,1,0:T(8,128)(2,1)S(1)}, bf16[2,128,512]{2,1,0:T(8,128)(2,1)S(1)}, bf16[2,128,512]{2,1,0:T(8,128)(2,1)S(1)}, bf16[2,128,512]{2,1,0:T(8,128)(2,1)S(1)}) fusion(bf16[1,2,128,1024]{3,2,1,0:T(8,128)(2,1)} %param.8, bf16[1,2,128,1024]{3,2,1,0:T(8,128)(2,1)} %param.7), kind=kLoop, calls=%fused_computation.2 | loop fusion | bytes 2097152 | tf_op jit(solution)/shard_map/squeeze | solution.py:200
  1.4 0.0 copy-start.2
  1.4 3.0 %collective-permute-start.4 = (bf16[4,128,512]{2,1,0:T(8,128)(2,1)S(1)}, bf16[4,128,512]{2,1,0:T(8,128)(2,1)S(1)}, u32[]{:S(2)}, u32[]{:S(2)}) collective-permute-start(bf16[4,128,512]{2,1,0:T(8,128)(2,1)S(1)} %pad_maximum_fusion.1.refs_0_), channel_id=1, source_target_pairs={{0,1},{1,0},{2,3},{3,2},{4,5},{5,4},{6,7},{7,6},{8,9},{9,8},{10,11... | collective-permute-start | bytes 1572872 | tf_op jit(solution)/shard_map/ppermute | solution.py:27
  4.4 1.6 %collective-permute-start.5 = (bf16[4,128,512]{2,1,0:T(8,128)(2,1)S(1)}, bf16[4,128,512]{2,1,0:T(8,128)(2,1)}, u32[]{:S(2)}, u32[]{:S(2)}) collective-permute-start(bf16[4,128,512]{2,1,0:T(8,128)(2,1)S(1)} %pad_maximum_fusion.1.refs_0_), channel_id=1, source_target_pairs={{0,2},{1,3},{2,4},{3,5},{4,6},{5,7},{6,0},{7,1},{8,10},{9,11},{10,... | collective-permute-start | bytes 1572872 | tf_op jit(solution)/shard_map/ppermute | solution.py:27
  6.0 0.0 copy-start.3
  6.0 0.6 collective-permute-start.1
  6.6 1.6 %collective-permute-start = (bf16[4,128,512]{2,1,0:T(8,128)(2,1)S(1)}, bf16[4,128,512]{2,1,0:T(8,128)(2,1)}, u32[]{:S(2)}, u32[]{:S(2)}) collective-permute-start(bf16[4,128,512]{2,1,0:T(8,128)(2,1)S(1)} %pad_maximum_fusion.refs_0_), channel_id=1, source_target_pairs={{0,2},{1,3},{2,4},{3,5},{4,6},{5,7},{6,0},{7,1},{8,10},{9,11},{10,... | collective-permute-start | bytes 1572872 | tf_op jit(solution)/shard_map/ppermute | solution.py:27
  8.2 0.0 collective-permute-start.10
  8.2 8.9 %collective-permute-done.4.__1_.refs_1_ = bf16[4,128,512]{2,1,0:T(8,128)(2,1)S(1)} collective-permute-done((bf16[4,128,512]{2,1,0:T(8,128)(2,1)S(1)}, bf16[4,128,512]{2,1,0:T(8,128)(2,1)S(1)}, u32[]{:S(2)}, u32[]{:S(2)}) %collective-permute-start.4) | collective-permute-done | bytes 524320 | tf_op jit(solution)/shard_map/ppermute | solution.py:27
  17.1 0.0 copy-start.4
  17.1 0.8 copy-done.4
  17.9 3.2 %collective-permute-done.5.__0_ = bf16[4,128,512]{2,1,0:T(8,128)(2,1)} collective-permute-done((bf16[4,128,512]{2,1,0:T(8,128)(2,1)S(1)}, bf16[4,128,512]{2,1,0:T(8,128)(2,1)}, u32[]{:S(2)}, u32[]{:S(2)}) %collective-permute-start.5) | collective-permute-done | bytes 524320 | tf_op jit(solution)/shard_map/ppermute | solution.py:27
  21.1 0.3 collective-permute-start.6
  21.4 0.2 collective-permute-start.11
  21.6 6.9 %collective-permute-done.1.__1_.refs_1_ = bf16[4,128,512]{2,1,0:T(8,128)(2,1)} collective-permute-done((bf16[4,128,512]{2,1,0:T(8,128)(2,1)S(1)}, bf16[4,128,512]{2,1,0:T(8,128)(2,1)}, u32[]{:S(2)}, u32[]{:S(2)}) %collective-permute-start.1) | collective-permute-done | bytes 524320 | tf_op jit(solution)/shard_map/ppermute | solution.py:27
  28.5 3.9 %collective-permute-done.__0_ = bf16[4,128,512]{2,1,0:T(8,128)(2,1)} collective-permute-done((bf16[4,128,512]{2,1,0:T(8,128)(2,1)S(1)}, bf16[4,128,512]{2,1,0:T(8,128)(2,1)}, u32[]{:S(2)}, u32[]{:S(2)}) %collective-permute-start) | collective-permute-done | bytes 524320 | tf_op jit(solution)/shard_map/ppermute | solution.py:27
  32.3 0.3 collective-permute-start.3
  32.6 0.0 collective-permute-start.2
  32.7 0.0 copy-done
  32.7 0.1 compare_reduce_fusion
  32.8 0.6 convert_element_type.3.live_ref
  33.4 6.3 %collective-permute-done.6.refs_3_.__1_ = bf16[4,128,512]{2,1,0:T(8,128)(2,1)} collective-permute-done((bf16[4,128,512]{2,1,0:T(8,128)(2,1)}, bf16[4,128,512]{2,1,0:T(8,128)(2,1)}, u32[]{:S(2)}, u32[]{:S(2)}) %collective-permute-start.6) | collective-permute-done | bytes 524320 | tf_op jit(solution)/shard_map/ppermute | solution.py:27
  39.7 3.9 %collective-permute-done.11.__0_ = bf16[4,128,512]{2,1,0:T(8,128)(2,1)} collective-permute-done((bf16[4,128,512]{2,1,0:T(8,128)(2,1)}, bf16[4,128,512]{2,1,0:T(8,128)(2,1)}, u32[]{:S(2)}, u32[]{:S(2)}) %collective-permute-start.11) | collective-permute-done | bytes 524320 | tf_op jit(solution)/shard_map/ppermute | solution.py:27
  43.6 0.3 collective-permute-start.12
  43.9 0.0 collective-permute-start.13
  43.9 0.0 copy-done.2
  43.9 10.1 %shard_map.57.__2_.refs_6_ = f32[2,2,128,4096]{3,2,1,0:T(8,128)} custom-call(s32[2,8,8]{2,1,0:T(8,128)} %convert_element_type.3.live_ref, bf16[2,128,8192]{2,1,0:T(8,128)(2,1)} %bitcast.14, bf16[4,128,512]{2,1,0:T(8,128)(2,1)} %copy-done.2, bf16[4,128,512]{2,1,0:T(8,128)(2,1)} %copy-done.4, bf16[4,128,512]{2,1,0:T(8,128)(2,1)} %shard_map.56.refs_2_, ...), custom_call_target="tpu_custom_call" | custom-call | tf_op jit(solution)/shard_map/pallas_call | solution.py:154
  54.0 0.0 copy-done.3
  54.0 0.0 collective-permute-done.3.__1_.refs_3_
  54.0 0.8 collective-permute-done.2.__0_
  54.8 1.0 collective-permute-start.7
  55.8 1.4 %collective-permute-start.8 = (bf16[4,128,512]{2,1,0:T(8,128)(2,1)}, bf16[4,128,512]{2,1,0:T(8,128)(2,1)S(1)}, u32[]{:S(2)}, u32[]{:S(2)}) collective-permute-start(bf16[4,128,512]{2,1,0:T(8,128)(2,1)} %shard_map.58.refs_1_), channel_id=1, source_target_pairs={{0,2},{1,3},{2,4},{3,5},{4,6},{5,7},{6,0},{7,1},{8,10},{9,11},{10,... | collective-permute-start | bytes 1572872 | tf_op jit(solution)/shard_map/ppermute | solution.py:27
  57.1 10.1 %shard_map.60.__2_.refs_6_ = f32[2,2,128,4096]{3,2,1,0:T(8,128)} custom-call(s32[2,8,8]{2,1,0:T(8,128)} %convert_element_type.3.live_ref, bf16[2,128,8192]{2,1,0:T(8,128)(2,1)} %bitcast.15, bf16[4,128,512]{2,1,0:T(8,128)(2,1)} %copy-done.3, bf16[4,128,512]{2,1,0:T(8,128)(2,1)} %collective-permute-done.1.__1_.refs_1_, ...), custom_call_target="tpu_custom_call" | custom-call | tf_op jit(solution)/shard_map/pallas_call | solution.py:154
  67.3 0.0 collective-permute-done.12.__1_.refs_2_
  67.3 0.0 collective-permute-done.13.__0_
  67.3 0.6 collective-permute-start.14
  67.9 5.4 %collective-permute-done.7.__1_.refs_2_ = bf16[4,128,512]{2,1,0:T(8,128)(2,1)S(1)} collective-permute-done((bf16[4,128,512]{2,1,0:T(8,128)(2,1)}, bf16[4,128,512]{2,1,0:T(8,128)(2,1)S(1)}, u32[]{:S(2)}, u32[]{:S(2)}) %collective-permute-start.7) | collective-permute-done | bytes 524320 | tf_op jit(solution)/shard_map/ppermute | solution.py:27
  73.3 0.0 copy-start.5
  73.3 2.5 %collective-permute-done.8.__0_ = bf16[4,128,512]{2,1,0:T(8,128)(2,1)S(1)} collective-permute-done((bf16[4,128,512]{2,1,0:T(8,128)(2,1)}, bf16[4,128,512]{2,1,0:T(8,128)(2,1)S(1)}, u32[]{:S(2)}, u32[]{:S(2)}) %collective-permute-start.8) | collective-permute-done | bytes 524320 | tf_op jit(solution)/shard_map/ppermute | solution.py:27
  75.8 0.0 copy-done.5
  75.8 0.0 copy-start.6
  75.8 0.8 copy-done.6
  76.6 0.5 collective-permute-start.9
  77.1 7.5 %collective-permute-done.14.refs_4_ = bf16[4,128,512]{2,1,0:T(8,128)(2,1)} collective-permute-done((bf16[4,128,512]{2,1,0:T(8,128)(2,1)}, bf16[4,128,512]{2,1,0:T(8,128)(2,1)}, u32[]{:S(2)}, u32[]{:S(2)}) %collective-permute-start.14) | collective-permute-done | bytes 524320 | tf_op jit(solution)/shard_map/ppermute | solution.py:27
  84.6 0.0 collective-permute-done.10.refs_5_.refs_7_
  84.6 0.0 copy-start.1
  84.6 1.3 %copy-done.1 = bf16[128,8192]{1,0:T(8,128)(2,1)} copy-done((bf16[128,8192]{1,0:T(8,128)(2,1)}, bf16[128,8192]{1,0:T(8,128)(2,1)S(1)}, u32[]{:S(2)}) %copy-start.1) | copy-done | bytes 2097176
  86.0 11.1 %shard_map.63.refs_7_ = f32[128,8192]{1,0:T(8,128)} custom-call(s32[2,8,8]{2,1,0:T(8,128)} %convert_element_type.3.live_ref, bf16[2,128,8192]{2,1,0:T(8,128)(2,1)} %bitcast.16, bf16[4,128,512]{2,1,0:T(8,128)(2,1)} %copy-done.2, bf16[4,128,512]{2,1,0:T(8,128)(2,1)} %shard_map.61.refs_1_, bf16[4,128,512]{2,1,0:T(8,128)(2,1)} %collective-permute-done.12.__1_.refs_2_, ...), custom_call_target="tpu_custom_call" | custom-call | tf_op jit(solution)/shard_map/pallas_call | solution.py:154
  97.0 0.0 collective-permute-done.9.refs_4_
  97.0 0.0 copy-start.7
  97.0 0.8 copy-done.7
  97.8 11.1 %shard_map.64 = f32[128,8192]{1,0:T(8,128)} custom-call(s32[2,8,8]{2,1,0:T(8,128)} %convert_element_type.3.live_ref, bf16[2,128,8192]{2,1,0:T(8,128)(2,1)} %bitcast.17, bf16[4,128,512]{2,1,0:T(8,128)(2,1)} %copy-done.3, bf16[4,128,512]{2,1,0:T(8,128)(2,1)} %shard_map.58.refs_1_, bf16[4,128,512]{2,1,0:T(8,128)(2,1)} %copy-done.5, ...), custom_call_target="tpu_custom_call", output_to_operand_aliasing={{}: (9, {})} | custom-call | tf_op jit(solution)/shard_map/pallas_call | solution.py:154
  (10 shorter events, 0.1 us)
Async XLA Ops:
  0.0 32.7 %copy-start = (s32[1,2,8,8,8]{4,3,2,1,0:T(8,128)S(1)}, s32[1,2,8,8,8]{4,3,2,1,0:T(8,128)}, u32[]{:S(2)}) copy-start(s32[1,2,8,8,8]{4,3,2,1,0:T(8,128)} %param.9) | copy-start | bytes 12292
  1.4 42.6 %copy-start.2 = (bf16[4,128,512]{2,1,0:T(8,128)(2,1)}, bf16[4,128,512]{2,1,0:T(8,128)(2,1)S(1)}, u32[]{:S(2)}) copy-start(bf16[4,128,512]{2,1,0:T(8,128)(2,1)S(1)} %pad_maximum_fusion.1.refs_0_) | copy-start | bytes 1572868
  1.4 15.8 %collective-permute-start.4 = (bf16[4,128,512]{2,1,0:T(8,128)(2,1)S(1)}, bf16[4,128,512]{2,1,0:T(8,128)(2,1)S(1)}, u32[]{:S(2)}, u32[]{:S(2)}) collective-permute-start(bf16[4,128,512]{2,1,0:T(8,128)(2,1)S(1)} %pad_maximum_fusion.1.refs_0_), channel_id=1, source_target_pairs={{0,1},{1,0},{2,3},{3,2},{4,5},{5,4},{6,7},{7,6},{8,9},{9,8},{10,11... | collective-permute-start | bytes 1572872 | tf_op jit(solution)/shard_map/ppermute | solution.py:27
  4.4 16.7 %collective-permute-start.5 = (bf16[4,128,512]{2,1,0:T(8,128)(2,1)S(1)}, bf16[4,128,512]{2,1,0:T(8,128)(2,1)}, u32[]{:S(2)}, u32[]{:S(2)}) collective-permute-start(bf16[4,128,512]{2,1,0:T(8,128)(2,1)S(1)} %pad_maximum_fusion.1.refs_0_), channel_id=1, source_target_pairs={{0,2},{1,3},{2,4},{3,5},{4,6},{5,7},{6,0},{7,1},{8,10},{9,11},{10,... | collective-permute-start | bytes 1572872 | tf_op jit(solution)/shard_map/ppermute | solution.py:27
  6.0 48.0 %copy-start.3 = (bf16[4,128,512]{2,1,0:T(8,128)(2,1)}, bf16[4,128,512]{2,1,0:T(8,128)(2,1)S(1)}, u32[]{:S(2)}) copy-start(bf16[4,128,512]{2,1,0:T(8,128)(2,1)S(1)} %pad_maximum_fusion.refs_0_) | copy-start | bytes 1572868
  6.0 22.5 %collective-permute-start.1 = (bf16[4,128,512]{2,1,0:T(8,128)(2,1)S(1)}, bf16[4,128,512]{2,1,0:T(8,128)(2,1)}, u32[]{:S(2)}, u32[]{:S(2)}) collective-permute-start(bf16[4,128,512]{2,1,0:T(8,128)(2,1)S(1)} %pad_maximum_fusion.refs_0_), channel_id=1, source_target_pairs={{0,1},{1,0},{2,3},{3,2},{4,5},{5,4},{6,7},{7,6},{8,9},{9,8},{10,11... | collective-permute-start | bytes 1572872 | tf_op jit(solution)/shard_map/ppermute | solution.py:27
  6.6 25.7 %collective-permute-start = (bf16[4,128,512]{2,1,0:T(8,128)(2,1)S(1)}, bf16[4,128,512]{2,1,0:T(8,128)(2,1)}, u32[]{:S(2)}, u32[]{:S(2)}) collective-permute-start(bf16[4,128,512]{2,1,0:T(8,128)(2,1)S(1)} %pad_maximum_fusion.refs_0_), channel_id=1, source_target_pairs={{0,2},{1,3},{2,4},{3,5},{4,6},{5,7},{6,0},{7,1},{8,10},{9,11},{10,... | collective-permute-start | bytes 1572872 | tf_op jit(solution)/shard_map/ppermute | solution.py:27
  8.2 76.5 %collective-permute-start.10 = (bf16[128,8192]{1,0:T(8,128)(2,1)}, bf16[128,8192]{1,0:T(8,128)(2,1)S(1)}, u32[]{:S(2)}, u32[]{:S(2)}) collective-permute-start(bf16[128,8192]{1,0:T(8,128)(2,1)} %bitcast.6), channel_id=1, source_target_pairs={{0,8},{8,16},{16,24},{24,0},{1,9},{9,17},{17,25},{25,1},{2,10},{10... | collective-permute-start | bytes 6291464 | tf_op jit(solution)/shard_map/ppermute | solution.py:27
  17.1 0.8 copy-start.4
  21.1 18.6 %collective-permute-start.6 = (bf16[4,128,512]{2,1,0:T(8,128)(2,1)}, bf16[4,128,512]{2,1,0:T(8,128)(2,1)}, u32[]{:S(2)}, u32[]{:S(2)}) collective-permute-start(bf16[4,128,512]{2,1,0:T(8,128)(2,1)} %shard_map.56.refs_2_), channel_id=1, source_target_pairs={{0,1},{1,0},{2,3},{3,2},{4,5},{5,4},{6,7},{7,6},{8,9},{9,8},{10,11... | collective-permute-start | bytes 1572872 | tf_op jit(solution)/shard_map/ppermute | solution.py:27
  21.4 22.2 %collective-permute-start.11 = (bf16[4,128,512]{2,1,0:T(8,128)(2,1)}, bf16[4,128,512]{2,1,0:T(8,128)(2,1)}, u32[]{:S(2)}, u32[]{:S(2)}) collective-permute-start(bf16[4,128,512]{2,1,0:T(8,128)(2,1)} %shard_map.56.refs_2_), channel_id=1, source_target_pairs={{0,2},{1,3},{2,4},{3,5},{4,6},{5,7},{6,0},{7,1},{8,10},{9,11},{10,... | collective-permute-start | bytes 1572872 | tf_op jit(solution)/shard_map/ppermute | solution.py:27
  32.3 21.6 %collective-permute-start.3 = (bf16[4,128,512]{2,1,0:T(8,128)(2,1)}, bf16[4,128,512]{2,1,0:T(8,128)(2,1)}, u32[]{:S(2)}, u32[]{:S(2)}) collective-permute-start(bf16[4,128,512]{2,1,0:T(8,128)(2,1)} %shard_map.55.refs_2_), channel_id=1, source_target_pairs={{0,1},{1,0},{2,3},{3,2},{4,5},{5,4},{6,7},{7,6},{8,9},{9,8},{10,11... | collective-permute-start | bytes 1572872 | tf_op jit(solution)/shard_map/ppermute | solution.py:27
  32.6 22.2 %collective-permute-start.2 = (bf16[4,128,512]{2,1,0:T(8,128)(2,1)}, bf16[4,128,512]{2,1,0:T(8,128)(2,1)}, u32[]{:S(2)}, u32[]{:S(2)}) collective-permute-start(bf16[4,128,512]{2,1,0:T(8,128)(2,1)} %shard_map.55.refs_2_), channel_id=1, source_target_pairs={{0,2},{1,3},{2,4},{3,5},{4,6},{5,7},{6,0},{7,1},{8,10},{9,11},{10,... | collective-permute-start | bytes 1572872 | tf_op jit(solution)/shard_map/ppermute | solution.py:27
  43.6 23.7 %collective-permute-start.12 = (bf16[4,128,512]{2,1,0:T(8,128)(2,1)}, bf16[4,128,512]{2,1,0:T(8,128)(2,1)}, u32[]{:S(2)}, u32[]{:S(2)}) collective-permute-start(bf16[4,128,512]{2,1,0:T(8,128)(2,1)} %shard_map.61.refs_1_), channel_id=1, source_target_pairs={{0,1},{1,0},{2,3},{3,2},{4,5},{5,4},{6,7},{7,6},{8,9},{9,8},{10,11... | collective-permute-start | bytes 1572872 | tf_op jit(solution)/shard_map/ppermute | solution.py:27
  43.9 23.4 %collective-permute-start.13 = (bf16[4,128,512]{2,1,0:T(8,128)(2,1)}, bf16[4,128,512]{2,1,0:T(8,128)(2,1)}, u32[]{:S(2)}, u32[]{:S(2)}) collective-permute-start(bf16[4,128,512]{2,1,0:T(8,128)(2,1)} %shard_map.61.refs_1_), channel_id=1, source_target_pairs={{0,2},{1,3},{2,4},{3,5},{4,6},{5,7},{6,0},{7,1},{8,10},{9,11},{10,... | collective-permute-start | bytes 1572872 | tf_op jit(solution)/shard_map/ppermute | solution.py:27
  54.8 18.5 %collective-permute-start.7 = (bf16[4,128,512]{2,1,0:T(8,128)(2,1)}, bf16[4,128,512]{2,1,0:T(8,128)(2,1)S(1)}, u32[]{:S(2)}, u32[]{:S(2)}) collective-permute-start(bf16[4,128,512]{2,1,0:T(8,128)(2,1)} %shard_map.58.refs_1_), channel_id=1, source_target_pairs={{0,1},{1,0},{2,3},{3,2},{4,5},{5,4},{6,7},{7,6},{8,9},{9,8},{10,11... | collective-permute-start | bytes 1572872 | tf_op jit(solution)/shard_map/ppermute | solution.py:27
  55.8 20.0 %collective-permute-start.8 = (bf16[4,128,512]{2,1,0:T(8,128)(2,1)}, bf16[4,128,512]{2,1,0:T(8,128)(2,1)S(1)}, u32[]{:S(2)}, u32[]{:S(2)}) collective-permute-start(bf16[4,128,512]{2,1,0:T(8,128)(2,1)} %shard_map.58.refs_1_), channel_id=1, source_target_pairs={{0,2},{1,3},{2,4},{3,5},{4,6},{5,7},{6,0},{7,1},{8,10},{9,11},{10,... | collective-permute-start | bytes 1572872 | tf_op jit(solution)/shard_map/ppermute | solution.py:27
  67.3 17.4 %collective-permute-start.14 = (bf16[4,128,512]{2,1,0:T(8,128)(2,1)}, bf16[4,128,512]{2,1,0:T(8,128)(2,1)}, u32[]{:S(2)}, u32[]{:S(2)}) collective-permute-start(bf16[4,128,512]{2,1,0:T(8,128)(2,1)} %shard_map.62.refs_3_), channel_id=1, source_target_pairs={{0,1},{1,0},{2,3},{3,2},{4,5},{5,4},{6,7},{7,6},{8,9},{9,8},{10,11... | collective-permute-start | bytes 1572872 | tf_op jit(solution)/shard_map/ppermute | solution.py:27
  73.3 2.5 %copy-start.5 = (bf16[4,128,512]{2,1,0:T(8,128)(2,1)}, bf16[4,128,512]{2,1,0:T(8,128)(2,1)S(1)}, u32[]{:S(2)}) copy-start(bf16[4,128,512]{2,1,0:T(8,128)(2,1)S(1)} %collective-permute-done.7.__1_.refs_2_) | copy-start | bytes 1572868
  75.8 0.8 copy-start.6
  76.6 20.4 %collective-permute-start.9 = (bf16[4,128,512]{2,1,0:T(8,128)(2,1)}, bf16[4,128,512]{2,1,0:T(8,128)(2,1)S(1)}, u32[]{:S(2)}, u32[]{:S(2)}) collective-permute-start(bf16[4,128,512]{2,1,0:T(8,128)(2,1)} %shard_map.59.refs_3_), channel_id=1, source_target_pairs={{0,1},{1,0},{2,3},{3,2},{4,5},{5,4},{6,7},{7,6},{8,9},{9,8},{10,11... | collective-permute-start | bytes 1572872 | tf_op jit(solution)/shard_map/ppermute | solution.py:27
  84.6 1.3 %copy-start.1 = (bf16[128,8192]{1,0:T(8,128)(2,1)}, bf16[128,8192]{1,0:T(8,128)(2,1)S(1)}, u32[]{:S(2)}) copy-start(bf16[128,8192]{1,0:T(8,128)(2,1)S(1)} %collective-permute-done.10.refs_5_.refs_7_) | copy-start | bytes 6291460
  97.0 0.8 copy-start.7

commit v3 on v2

--- a/solution.py
+++ b/solution.py
@@ -47,11 +47,11 @@
     resumes, ends = stage in ("next", "last"), stage in ("whole", "last")
     refs = list(refs)
     carried_ref = refs.pop(0) if ends else None
-    before_ref = refs.pop(0) if resumes else None
+    means_before, logs_before = (refs.pop(0), refs.pop(0)) if resumes else (None, None)
     if ends:
         _, out_ref = refs
     else:
-        (sums_ref,) = refs
+        means_ref, logs_ref = refs
     tokens = q_ref.shape[1]
     group = pl.program_id(0)
     factor = math.log2(math.e) / math.sqrt(HD)
@@ -92,7 +92,7 @@
                 scores = jnp.concatenate([own_scores, scores[:, tokens:]], axis=1)
             row_max = jnp.max(scores, axis=1, keepdims=True)
             if resumes:
-                max_before = before_ref[1, layer, :, lanes]
+                max_before = logs_before[layer, :, lanes]
                 row_max = jnp.maximum(row_max, max_before)
                 shrink = jnp.exp2((max_before - row_max) * factor)
                 scores = scores - jnp.concatenate([row_max] * (scores.shape[1] // HD), axis=1)
@@ -102,11 +102,11 @@
             mixed = jnp.dot(weight, values, preferred_element_type=jnp.float32)
             mixed, total = mixed[:, :HD], mixed[:, HD:]
             if resumes:
-                mixed = before_ref[0, layer, :, lanes] * shrink + mixed
+                mixed = means_before[layer, :, lanes].astype(jnp.float32) * shrink + mixed
                 total = shrink + total
             if not ends:
-                sums_ref[0, layer, :, lanes] = mixed / total
-                sums_ref[1, layer, :, lanes] = row_max + jnp.log2(total) / factor
+                means_ref[layer, :, lanes] = (mixed / total).astype(means_ref.dtype)
+                logs_ref[layer, :, lanes] = row_max + jnp.log2(total) * (1.0 / factor)
                 continue
             attended = (mixed / total).astype(jnp.bfloat16).astype(jnp.float32)
             if layer:
@@ -122,7 +122,7 @@
     lanes = width // HK
     anywhere = pl.BlockSpec(memory_space=pl.ANY)
     columns = pl.BlockSpec((tokens, lanes), lambda g, _: (0, first_head + g))
-    sums = pl.BlockSpec((2, layers, tokens, lanes), lambda g, _: (0, 0, 0, g))
+    state = pl.BlockSpec((layers, tokens, lanes), lambda g, _: (0, 0, g))
     arrays, places = [], []
     for place, (array, base) in blocks.items():
         if not any(array is other for other in arrays):
@@ -139,8 +139,8 @@
         operands.append(carried)
         in_specs.append(columns)
     if before is not None:
-        operands.append(before)
-        in_specs.append(sums)
+        operands += before
+        in_specs += [state] * 2
     if ends:
         if out is not None:
             aliases = {len(operands): 0}
@@ -149,8 +149,11 @@
         out_specs = columns
         out_shape = jax.ShapeDtypeStruct((tokens, width), jnp.float32)
     else:
-        out_specs = sums
-        out_shape = jax.ShapeDtypeStruct((2, layers, tokens, lanes * heads), jnp.float32)
+        out_specs = [state] * 2
+        out_shape = [
+            jax.ShapeDtypeStruct((layers, tokens, lanes * heads), dtype)
+            for dtype in (jnp.bfloat16, jnp.float32)
+        ]
     return pl.pallas_call(
         functools.partial(attend_body, stage, layers, first_head, tuple(places)),
         grid_spec=pltpu.PrefetchScalarGridSpec(
@@ -214,13 +217,15 @@
 
     states = [None, None]
     for step in range(rows):
-        streams[0].go(step, [states[1]] if step == rows - 1 else [])
+        streams[0].go(step, states[1] if step == rows - 1 else [])
         if step + 1 == cut:
             states[0] = attended("first", 0, range(cut))
-        streams[1].go(step, [states[0]] if step == rows - 2 else [])
+        if step == rows - 1:
+            states[0] = attended("next", 0, range(cut, rows - 1), states[0])
+        streams[1].go(step, states[0] if step >= rows - 2 else [])
         if step + 1 == cut:
             states[1] = attended("first", 1, range(cut))
-    out = attended("last", 0, range(cut, rows), states[0])
+    out = attended("last", 0, range(rows - 1, rows), states[0])
     out = attended("last", 1, range(cut, rows), states[1], out)
     return out[None]
 

time: 109 us -> 109 us (level)
  waiting for transfers between devices: 49.3 us -> 34.4 us
  starting transfers between devices: 11.3 us -> 19.6 us
  Pallas kernels: 42.3 us -> 49.1 us
  local copies, waits for them, and re-layouts: 5.02 us -> 3.9 us
    ppermute x15, waiting for transfers between devices: 49.3 us -> 34.4 us  [rotated(): return lax.ppermute(array, axis, [(i, move(i)) for i in range(size)])]
    ppermute x15, starting transfers between devices: 11.3 us -> 19.6 us  [rotated(): return lax.ppermute(array, axis, [(i, move(i)) for i in range(size)])]
    pallas_call x4 -> x5, Pallas kernels: 42.3 us -> 49.1 us  [attend(): pl.pallas_call(functools.partial(attend_body, stage, layers, first_head,...]
    unnamed x16, local copies, waits for them, and re-layouts: 3.72 us -> 2.6 us
  transfers between devices with their start and end apart: 15 -> 15, of which waited for: 10 -> 6; matrix products, arithmetic and copies ran while one was open for 1% -> 1% of each run, Pallas kernels for 29% -> 36%
where the time goes in v3:
time: 109 us; the launch traced here: 108 us
  Pallas kernels  49.1 us (45%)
  waiting for transfers between devices  34.4 us (32%)
  starting transfers between devices  19.6 us (18%)
  local copies, waits for them, and re-layouts  3.9 us (4%)
    pallas_call x5, Pallas kernels, attend(): pl.pallas_call(functools.partial(attend_body, stage, layers, first_head,...  49.1 us
    ppermute x15, waiting for transfers between devices, rotated(): return lax.ppermute(array, axis, [(i, move(i)) for i in range(size)])  34.4 us
    ppermute x15, starting transfers between devices, rotated(): return lax.ppermute(array, axis, [(i, move(i)) for i in range(size)])  19.6 us
    unnamed x16, local copies, waits for them, and re-layouts  2.6 us
  transfers between devices with their start and end apart: 15, of which 6 were waited for; matrix products, arithmetic and copies ran while one was open for 1% of the time, Pallas kernels for 36%

profile of v3, /device:TPU:0, one launch (start us, length us, event | category | flops | bytes accessed | tf_op | source)
XLA Modules:
  0.0 107.9 jit_solution(1909412860192407072)
XLA Ops:
  0.0 0.0 copy-start
  0.0 1.3 %slice_bitcast_fusion = (bf16[2,128,512]{2,1,0:T(8,128)(2,1)S(1)}, bf16[2,128,512]{2,1,0:T(8,128)(2,1)S(1)}, bf16[2,128,512]{2,1,0:T(8,128)(2,1)S(1)}, bf16[2,128,512]{2,1,0:T(8,128)(2,1)S(1)}) fusion(bf16[1,2,128,1024]{3,2,1,0:T(8,128)(2,1)} %param.8, bf16[1,2,128,1024]{3,2,1,0:T(8,128)(2,1)} %param.7), kind=kLoop, calls=%fused_computation.2 | loop fusion | bytes 2097152 | tf_op jit(solution)/shard_map/squeeze | solution.py:203
  1.4 0.0 copy-start.2
  1.4 3.1 %collective-permute-start.5 = (bf16[4,128,512]{2,1,0:T(8,128)(2,1)S(1)}, bf16[4,128,512]{2,1,0:T(8,128)(2,1)S(1)}, u32[]{:S(2)}, u32[]{:S(2)}) collective-permute-start(bf16[4,128,512]{2,1,0:T(8,128)(2,1)S(1)} %pad_maximum_fusion.1.refs_0_), channel_id=1, source_target_pairs={{0,2},{1,3},{2,4},{3,5},{4,6},{5,7},{6,0},{7,1},{8,10},{9,11},{10,... | collective-permute-start | bytes 1572872 | tf_op jit(solution)/shard_map/ppermute | solution.py:27
  4.4 1.5 %collective-permute-start.4 = (bf16[4,128,512]{2,1,0:T(8,128)(2,1)S(1)}, bf16[4,128,512]{2,1,0:T(8,128)(2,1)}, u32[]{:S(2)}, u32[]{:S(2)}) collective-permute-start(bf16[4,128,512]{2,1,0:T(8,128)(2,1)S(1)} %pad_maximum_fusion.1.refs_0_), channel_id=1, source_target_pairs={{0,1},{1,0},{2,3},{3,2},{4,5},{5,4},{6,7},{7,6},{8,9},{9,8},{10,11... | collective-permute-start | bytes 1572872 | tf_op jit(solution)/shard_map/ppermute | solution.py:27
  6.0 0.0 copy-start.3
  6.0 0.6 collective-permute-start.1
  6.6 1.6 %collective-permute-start = (bf16[4,128,512]{2,1,0:T(8,128)(2,1)S(1)}, bf16[4,128,512]{2,1,0:T(8,128)(2,1)}, u32[]{:S(2)}, u32[]{:S(2)}) collective-permute-start(bf16[4,128,512]{2,1,0:T(8,128)(2,1)S(1)} %pad_maximum_fusion.refs_0_), channel_id=1, source_target_pairs={{0,2},{1,3},{2,4},{3,5},{4,6},{5,7},{6,0},{7,1},{8,10},{9,11},{10,... | collective-permute-start | bytes 1572872 | tf_op jit(solution)/shard_map/ppermute | solution.py:27
  8.2 0.0 collective-permute-start.12
  8.2 11.0 %collective-permute-done.5.__0_ = bf16[4,128,512]{2,1,0:T(8,128)(2,1)S(1)} collective-permute-done((bf16[4,128,512]{2,1,0:T(8,128)(2,1)S(1)}, bf16[4,128,512]{2,1,0:T(8,128)(2,1)S(1)}, u32[]{:S(2)}, u32[]{:S(2)}) %collective-permute-start.5) | collective-permute-done | bytes 524320 | tf_op jit(solution)/shard_map/ppermute | solution.py:27
  19.2 0.0 copy-start.4
  19.2 0.8 copy-done.4
  20.0 0.0 collective-permute-done.4.__1_.refs_1_
  20.0 0.9 collective-permute-start.9
  21.0 1.5 %collective-permute-start.6 = (bf16[4,128,512]{2,1,0:T(8,128)(2,1)}, bf16[4,128,512]{2,1,0:T(8,128)(2,1)}, u32[]{:S(2)}, u32[]{:S(2)}) collective-permute-start(bf16[4,128,512]{2,1,0:T(8,128)(2,1)} %shard_map.56.refs_2_), channel_id=1, source_target_pairs={{0,1},{1,0},{2,3},{3,2},{4,5},{5,4},{6,7},{7,6},{8,9},{9,8},{10,11... | collective-permute-start | bytes 1572872 | tf_op jit(solution)/shard_map/ppermute | solution.py:27
  22.5 8.2 %collective-permute-done.1.__1_.refs_1_ = bf16[4,128,512]{2,1,0:T(8,128)(2,1)} collective-permute-done((bf16[4,128,512]{2,1,0:T(8,128)(2,1)S(1)}, bf16[4,128,512]{2,1,0:T(8,128)(2,1)}, u32[]{:S(2)}, u32[]{:S(2)}) %collective-permute-start.1) | collective-permute-done | bytes 524320 | tf_op jit(solution)/shard_map/ppermute | solution.py:27
  30.6 0.0 collective-permute-done.__0_
  30.6 1.7 %collective-permute-start.3 = (bf16[4,128,512]{2,1,0:T(8,128)(2,1)}, bf16[4,128,512]{2,1,0:T(8,128)(2,1)}, u32[]{:S(2)}, u32[]{:S(2)}) collective-permute-start(bf16[4,128,512]{2,1,0:T(8,128)(2,1)} %shard_map.55.refs_2_), channel_id=1, source_target_pairs={{0,1},{1,0},{2,3},{3,2},{4,5},{5,4},{6,7},{7,6},{8,9},{9,8},{10,11... | collective-permute-start | bytes 1572872 | tf_op jit(solution)/shard_map/ppermute | solution.py:27
  32.3 1.4 %collective-permute-start.2 = (bf16[4,128,512]{2,1,0:T(8,128)(2,1)}, bf16[4,128,512]{2,1,0:T(8,128)(2,1)}, u32[]{:S(2)}, u32[]{:S(2)}) collective-permute-start(bf16[4,128,512]{2,1,0:T(8,128)(2,1)} %shard_map.55.refs_2_), channel_id=1, source_target_pairs={{0,2},{1,3},{2,4},{3,5},{4,6},{5,7},{6,0},{7,1},{8,10},{9,11},{10,... | collective-permute-start | bytes 1572872 | tf_op jit(solution)/shard_map/ppermute | solution.py:27
  33.7 0.0 copy-done
  33.7 0.1 compare_reduce_fusion
  33.8 0.6 convert_element_type.3.live_ref
  34.5 7.3 %collective-permute-done.9.__0_ = bf16[4,128,512]{2,1,0:T(8,128)(2,1)} collective-permute-done((bf16[4,128,512]{2,1,0:T(8,128)(2,1)}, bf16[4,128,512]{2,1,0:T(8,128)(2,1)}, u32[]{:S(2)}, u32[]{:S(2)}) %collective-permute-start.9) | collective-permute-done | bytes 524320 | tf_op jit(solution)/shard_map/ppermute | solution.py:27
  41.8 0.1 collective-permute-done.6.refs_3_.__1_
  41.9 1.6 %collective-permute-start.13 = (bf16[4,128,512]{2,1,0:T(8,128)(2,1)}, bf16[4,128,512]{2,1,0:T(8,128)(2,1)}, u32[]{:S(2)}, u32[]{:S(2)}) collective-permute-start(bf16[4,128,512]{2,1,0:T(8,128)(2,1)} %shard_map.59.refs_1_), channel_id=1, source_target_pairs={{0,2},{1,3},{2,4},{3,5},{4,6},{5,7},{6,0},{7,1},{8,10},{9,11},{10,... | collective-permute-start | bytes 1572872 | tf_op jit(solution)/shard_map/ppermute | solution.py:27
  43.4 1.5 %collective-permute-start.10 = (bf16[4,128,512]{2,1,0:T(8,128)(2,1)}, bf16[4,128,512]{2,1,0:T(8,128)(2,1)}, u32[]{:S(2)}, u32[]{:S(2)}) collective-permute-start(bf16[4,128,512]{2,1,0:T(8,128)(2,1)} %shard_map.59.refs_1_), channel_id=1, source_target_pairs={{0,1},{1,0},{2,3},{3,2},{4,5},{5,4},{6,7},{7,6},{8,9},{9,8},{10,11... | collective-permute-start | bytes 1572872 | tf_op jit(solution)/shard_map/ppermute | solution.py:27
  44.9 0.0 copy-done.2
  44.9 9.7 %shard_map.57 = (bf16[2,128,4096]{2,1,0:T(8,128)(2,1)}, f32[2,128,4096]{2,1,0:T(8,128)}) custom-call(s32[2,8,8]{2,1,0:T(8,128)} %convert_element_type.3.live_ref, bf16[2,128,8192]{2,1,0:T(8,128)(2,1)} %bitcast.14, bf16[4,128,512]{2,1,0:T(8,128)(2,1)} %copy-done.2, bf16[4,128,512]{2,1,0:T(8,128)(2,1)} %collective-permute-done.4.__1_.refs_1_, ...), custom_call_target="tpu_custom_call" | custom-call | tf_op jit(solution)/shard_map/pallas_call | solution.py:157
  54.7 0.0 copy-done.3
  54.7 0.0 collective-permute-done.3.__1_.refs_3_
  54.7 0.0 collective-permute-done.2.__0_
  54.7 1.6 %collective-permute-start.8 = (bf16[4,128,512]{2,1,0:T(8,128)(2,1)}, bf16[4,128,512]{2,1,0:T(8,128)(2,1)S(1)}, u32[]{:S(2)}, u32[]{:S(2)}) collective-permute-start(bf16[4,128,512]{2,1,0:T(8,128)(2,1)} %shard_map.58.refs_1_), channel_id=1, source_target_pairs={{0,2},{1,3},{2,4},{3,5},{4,6},{5,7},{6,0},{7,1},{8,10},{9,11},{10,... | collective-permute-start | bytes 1572872 | tf_op jit(solution)/shard_map/ppermute | solution.py:27
  56.3 0.5 collective-permute-start.7
  56.9 9.8 %shard_map.62 = (bf16[2,128,4096]{2,1,0:T(8,128)(2,1)}, f32[2,128,4096]{2,1,0:T(8,128)}) custom-call(s32[2,8,8]{2,1,0:T(8,128)} %convert_element_type.3.live_ref, bf16[2,128,8192]{2,1,0:T(8,128)(2,1)} %bitcast.15, bf16[4,128,512]{2,1,0:T(8,128)(2,1)} %copy-done.3, bf16[4,128,512]{2,1,0:T(8,128)(2,1)} %collective-permute-done.1.__1_.refs_1_, ...), custom_call_target="tpu_custom_call" | custom-call | tf_op jit(solution)/shard_map/pallas_call | solution.py:157
  66.7 0.0 collective-permute-done.13.__0_
  66.7 0.0 collective-permute-done.10.refs_2_.__1_
  66.7 1.6 %collective-permute-start.14 = (bf16[4,128,512]{2,1,0:T(8,128)(2,1)}, bf16[4,128,512]{2,1,0:T(8,128)(2,1)}, u32[]{:S(2)}, u32[]{:S(2)}) collective-permute-start(bf16[4,128,512]{2,1,0:T(8,128)(2,1)} %shard_map.63.refs_1_), channel_id=1, source_target_pairs={{0,1},{1,0},{2,3},{3,2},{4,5},{5,4},{6,7},{7,6},{8,9},{9,8},{10,11... | collective-permute-start | bytes 1572872 | tf_op jit(solution)/shard_map/ppermute | solution.py:27
  68.3 10.0 %shard_map.60 = (bf16[2,128,4096]{2,1,0:T(8,128)(2,1)}, f32[2,128,4096]{2,1,0:T(8,128)}) custom-call(s32[2,8,8]{2,1,0:T(8,128)} %convert_element_type.3.live_ref, bf16[2,128,8192]{2,1,0:T(8,128)(2,1)} %bitcast.16, bf16[4,128,512]{2,1,0:T(8,128)(2,1)} %copy-done.2, bf16[4,128,512]{2,1,0:T(8,128)(2,1)} %shard_map.59.refs_1_, ...), custom_call_target="tpu_custom_call" | custom-call | tf_op jit(solution)/shard_map/pallas_call | solution.py:157
  78.3 0.0 collective-permute-done.8.__0_
  78.3 0.0 copy-start.6
  78.4 0.0 collective-permute-done.7.__1_.refs_2_
  78.4 0.0 copy-start.5
  78.4 0.8 copy-done.6
  79.1 0.2 copy-done.5
  79.3 0.5 collective-permute-start.11
  79.9 0.0 collective-permute-done.12.refs_3_.refs_6_.refs_5_
  79.9 0.0 copy-start.1
  79.9 6.9 %collective-permute-done.14.refs_2_ = bf16[4,128,512]{2,1,0:T(8,128)(2,1)} collective-permute-done((bf16[4,128,512]{2,1,0:T(8,128)(2,1)}, bf16[4,128,512]{2,1,0:T(8,128)(2,1)}, u32[]{:S(2)}, u32[]{:S(2)}) %collective-permute-start.14) | collective-permute-done | bytes 524320 | tf_op jit(solution)/shard_map/ppermute | solution.py:27
  86.8 0.0 copy-done.1
  86.8 8.8 %shard_map.64.refs_8_ = f32[128,8192]{1,0:T(8,128)} custom-call(s32[2,8,8]{2,1,0:T(8,128)} %convert_element_type.3.live_ref, bf16[2,128,8192]{2,1,0:T(8,128)(2,1)} %bitcast.17, bf16[4,128,512]{2,1,0:T(8,128)(2,1)} %copy-done.2, bf16[4,128,512]{2,1,0:T(8,128)(2,1)} %shard_map.63.refs_1_, bf16[4,128,512]{2,1,0:T(8,128)(2,1)} %collective-permute-done.14.refs_2_, ...), custom_call_target="tpu_custom_call" | custom-call | tf_op jit(solution)/shard_map/pallas_call | solution.py:157
  95.7 0.8 collective-permute-done.11.refs_4_
  96.5 0.0 copy-start.7
  96.5 0.8 copy-done.7
  97.3 10.6 %shard_map.65 = f32[128,8192]{1,0:T(8,128)} custom-call(s32[2,8,8]{2,1,0:T(8,128)} %convert_element_type.3.live_ref, bf16[2,128,8192]{2,1,0:T(8,128)(2,1)} %bitcast.18, bf16[4,128,512]{2,1,0:T(8,128)(2,1)} %copy-done.3, bf16[4,128,512]{2,1,0:T(8,128)(2,1)} %shard_map.58.refs_1_, bf16[4,128,512]{2,1,0:T(8,128)(2,1)} %copy-done.5, ...), custom_call_target="tpu_custom_call", output_to_operand_aliasing={{}: (10, {})} | custom-call | tf_op jit(solution)/shard_map/pallas_call | solution.py:157
  (10 shorter events, 0.1 us)
Async XLA Ops:
  0.0 33.7 %copy-start = (s32[1,2,8,8,8]{4,3,2,1,0:T(8,128)S(1)}, s32[1,2,8,8,8]{4,3,2,1,0:T(8,128)}, u32[]{:S(2)}) copy-start(s32[1,2,8,8,8]{4,3,2,1,0:T(8,128)} %param.9) | copy-start | bytes 12292
  1.4 43.6 %copy-start.2 = (bf16[4,128,512]{2,1,0:T(8,128)(2,1)}, bf16[4,128,512]{2,1,0:T(8,128)(2,1)S(1)}, u32[]{:S(2)}) copy-start(bf16[4,128,512]{2,1,0:T(8,128)(2,1)S(1)} %pad_maximum_fusion.1.refs_0_) | copy-start | bytes 1572868
  1.4 17.9 %collective-permute-start.5 = (bf16[4,128,512]{2,1,0:T(8,128)(2,1)S(1)}, bf16[4,128,512]{2,1,0:T(8,128)(2,1)S(1)}, u32[]{:S(2)}, u32[]{:S(2)}) collective-permute-start(bf16[4,128,512]{2,1,0:T(8,128)(2,1)S(1)} %pad_maximum_fusion.1.refs_0_), channel_id=1, source_target_pairs={{0,2},{1,3},{2,4},{3,5},{4,6},{5,7},{6,0},{7,1},{8,10},{9,11},{10,... | collective-permute-start | bytes 1572872 | tf_op jit(solution)/shard_map/ppermute | solution.py:27
  4.4 15.6 %collective-permute-start.4 = (bf16[4,128,512]{2,1,0:T(8,128)(2,1)S(1)}, bf16[4,128,512]{2,1,0:T(8,128)(2,1)}, u32[]{:S(2)}, u32[]{:S(2)}) collective-permute-start(bf16[4,128,512]{2,1,0:T(8,128)(2,1)S(1)} %pad_maximum_fusion.1.refs_0_), channel_id=1, source_target_pairs={{0,1},{1,0},{2,3},{3,2},{4,5},{5,4},{6,7},{7,6},{8,9},{9,8},{10,11... | collective-permute-start | bytes 1572872 | tf_op jit(solution)/shard_map/ppermute | solution.py:27
  6.0 48.7 %copy-start.3 = (bf16[4,128,512]{2,1,0:T(8,128)(2,1)}, bf16[4,128,512]{2,1,0:T(8,128)(2,1)S(1)}, u32[]{:S(2)}) copy-start(bf16[4,128,512]{2,1,0:T(8,128)(2,1)S(1)} %pad_maximum_fusion.refs_0_) | copy-start | bytes 1572868
  6.0 24.6 %collective-permute-start.1 = (bf16[4,128,512]{2,1,0:T(8,128)(2,1)S(1)}, bf16[4,128,512]{2,1,0:T(8,128)(2,1)}, u32[]{:S(2)}, u32[]{:S(2)}) collective-permute-start(bf16[4,128,512]{2,1,0:T(8,128)(2,1)S(1)} %pad_maximum_fusion.refs_0_), channel_id=1, source_target_pairs={{0,1},{1,0},{2,3},{3,2},{4,5},{5,4},{6,7},{7,6},{8,9},{9,8},{10,11... | collective-permute-start | bytes 1572872 | tf_op jit(solution)/shard_map/ppermute | solution.py:27
  6.6 24.0 %collective-permute-start = (bf16[4,128,512]{2,1,0:T(8,128)(2,1)S(1)}, bf16[4,128,512]{2,1,0:T(8,128)(2,1)}, u32[]{:S(2)}, u32[]{:S(2)}) collective-permute-start(bf16[4,128,512]{2,1,0:T(8,128)(2,1)S(1)} %pad_maximum_fusion.refs_0_), channel_id=1, source_target_pairs={{0,2},{1,3},{2,4},{3,5},{4,6},{5,7},{6,0},{7,1},{8,10},{9,11},{10,... | collective-permute-start | bytes 1572872 | tf_op jit(solution)/shard_map/ppermute | solution.py:27
  8.2 71.7 %collective-permute-start.12 = (bf16[128,8192]{1,0:T(8,128)(2,1)}, bf16[128,8192]{1,0:T(8,128)(2,1)S(1)}, u32[]{:S(2)}, u32[]{:S(2)}) collective-permute-start(bf16[128,8192]{1,0:T(8,128)(2,1)} %bitcast.6), channel_id=1, source_target_pairs={{0,8},{8,16},{16,24},{24,0},{1,9},{9,17},{17,25},{25,1},{2,10},{10... | collective-permute-start | bytes 6291464 | tf_op jit(solution)/shard_map/ppermute | solution.py:27
  19.2 0.8 copy-start.4
  20.0 21.8 %collective-permute-start.9 = (bf16[4,128,512]{2,1,0:T(8,128)(2,1)}, bf16[4,128,512]{2,1,0:T(8,128)(2,1)}, u32[]{:S(2)}, u32[]{:S(2)}) collective-permute-start(bf16[4,128,512]{2,1,0:T(8,128)(2,1)} %shard_map.56.refs_2_), channel_id=1, source_target_pairs={{0,2},{1,3},{2,4},{3,5},{4,6},{5,7},{6,0},{7,1},{8,10},{9,11},{10,... | collective-permute-start | bytes 1572872 | tf_op jit(solution)/shard_map/ppermute | solution.py:27
  21.0 20.9 %collective-permute-start.6 = (bf16[4,128,512]{2,1,0:T(8,128)(2,1)}, bf16[4,128,512]{2,1,0:T(8,128)(2,1)}, u32[]{:S(2)}, u32[]{:S(2)}) collective-permute-start(bf16[4,128,512]{2,1,0:T(8,128)(2,1)} %shard_map.56.refs_2_), channel_id=1, source_target_pairs={{0,1},{1,0},{2,3},{3,2},{4,5},{5,4},{6,7},{7,6},{8,9},{9,8},{10,11... | collective-permute-start | bytes 1572872 | tf_op jit(solution)/shard_map/ppermute | solution.py:27
  30.6 24.1 %collective-permute-start.3 = (bf16[4,128,512]{2,1,0:T(8,128)(2,1)}, bf16[4,128,512]{2,1,0:T(8,128)(2,1)}, u32[]{:S(2)}, u32[]{:S(2)}) collective-permute-start(bf16[4,128,512]{2,1,0:T(8,128)(2,1)} %shard_map.55.refs_2_), channel_id=1, source_target_pairs={{0,1},{1,0},{2,3},{3,2},{4,5},{5,4},{6,7},{7,6},{8,9},{9,8},{10,11... | collective-permute-start | bytes 1572872 | tf_op jit(solution)/shard_map/ppermute | solution.py:27
  32.3 22.4 %collective-permute-start.2 = (bf16[4,128,512]{2,1,0:T(8,128)(2,1)}, bf16[4,128,512]{2,1,0:T(8,128)(2,1)}, u32[]{:S(2)}, u32[]{:S(2)}) collective-permute-start(bf16[4,128,512]{2,1,0:T(8,128)(2,1)} %shard_map.55.refs_2_), channel_id=1, source_target_pairs={{0,2},{1,3},{2,4},{3,5},{4,6},{5,7},{6,0},{7,1},{8,10},{9,11},{10,... | collective-permute-start | bytes 1572872 | tf_op jit(solution)/shard_map/ppermute | solution.py:27
  41.9 24.9 %collective-permute-start.13 = (bf16[4,128,512]{2,1,0:T(8,128)(2,1)}, bf16[4,128,512]{2,1,0:T(8,128)(2,1)}, u32[]{:S(2)}, u32[]{:S(2)}) collective-permute-start(bf16[4,128,512]{2,1,0:T(8,128)(2,1)} %shard_map.59.refs_1_), channel_id=1, source_target_pairs={{0,2},{1,3},{2,4},{3,5},{4,6},{5,7},{6,0},{7,1},{8,10},{9,11},{10,... | collective-permute-start | bytes 1572872 | tf_op jit(solution)/shard_map/ppermute | solution.py:27
  43.4 23.3 %collective-permute-start.10 = (bf16[4,128,512]{2,1,0:T(8,128)(2,1)}, bf16[4,128,512]{2,1,0:T(8,128)(2,1)}, u32[]{:S(2)}, u32[]{:S(2)}) collective-permute-start(bf16[4,128,512]{2,1,0:T(8,128)(2,1)} %shard_map.59.refs_1_), channel_id=1, source_target_pairs={{0,1},{1,0},{2,3},{3,2},{4,5},{5,4},{6,7},{7,6},{8,9},{9,8},{10,11... | collective-permute-start | bytes 1572872 | tf_op jit(solution)/shard_map/ppermute | solution.py:27
  54.7 23.6 %collective-permute-start.8 = (bf16[4,128,512]{2,1,0:T(8,128)(2,1)}, bf16[4,128,512]{2,1,0:T(8,128)(2,1)S(1)}, u32[]{:S(2)}, u32[]{:S(2)}) collective-permute-start(bf16[4,128,512]{2,1,0:T(8,128)(2,1)} %shard_map.58.refs_1_), channel_id=1, source_target_pairs={{0,2},{1,3},{2,4},{3,5},{4,6},{5,7},{6,0},{7,1},{8,10},{9,11},{10,... | collective-permute-start | bytes 1572872 | tf_op jit(solution)/shard_map/ppermute | solution.py:27
  56.3 22.0 %collective-permute-start.7 = (bf16[4,128,512]{2,1,0:T(8,128)(2,1)}, bf16[4,128,512]{2,1,0:T(8,128)(2,1)S(1)}, u32[]{:S(2)}, u32[]{:S(2)}) collective-permute-start(bf16[4,128,512]{2,1,0:T(8,128)(2,1)} %shard_map.58.refs_1_), channel_id=1, source_target_pairs={{0,1},{1,0},{2,3},{3,2},{4,5},{5,4},{6,7},{7,6},{8,9},{9,8},{10,11... | collective-permute-start | bytes 1572872 | tf_op jit(solution)/shard_map/ppermute | solution.py:27
  66.7 20.1 %collective-permute-start.14 = (bf16[4,128,512]{2,1,0:T(8,128)(2,1)}, bf16[4,128,512]{2,1,0:T(8,128)(2,1)}, u32[]{:S(2)}, u32[]{:S(2)}) collective-permute-start(bf16[4,128,512]{2,1,0:T(8,128)(2,1)} %shard_map.63.refs_1_), channel_id=1, source_target_pairs={{0,1},{1,0},{2,3},{3,2},{4,5},{5,4},{6,7},{7,6},{8,9},{9,8},{10,11... | collective-permute-start | bytes 1572872 | tf_op jit(solution)/shard_map/ppermute | solution.py:27
  78.3 0.8 copy-start.6
  78.4 1.0 copy-start.5
  79.3 17.1 %collective-permute-start.11 = (bf16[4,128,512]{2,1,0:T(8,128)(2,1)}, bf16[4,128,512]{2,1,0:T(8,128)(2,1)S(1)}, u32[]{:S(2)}, u32[]{:S(2)}) collective-permute-start(bf16[4,128,512]{2,1,0:T(8,128)(2,1)} %shard_map.61.refs_3_), channel_id=1, source_target_pairs={{0,1},{1,0},{2,3},{3,2},{4,5},{5,4},{6,7},{7,6},{8,9},{9,8},{10,11... | collective-permute-start | bytes 1572872 | tf_op jit(solution)/shard_map/ppermute | solution.py:27
  79.9 6.9 %copy-start.1 = (bf16[128,8192]{1,0:T(8,128)(2,1)}, bf16[128,8192]{1,0:T(8,128)(2,1)S(1)}, u32[]{:S(2)}) copy-start(bf16[128,8192]{1,0:T(8,128)(2,1)S(1)} %collective-permute-done.12.refs_3_.refs_6_.refs_5_) | copy-start | bytes 6291460
  96.5 0.8 copy-start.7
